TPU v7x, 32 devices: a whole 2x2x4 slice. The times are simulated.
32 devices in a mesh: grp: 2 (over x), scen: 8 (over z, y), bund: 2 (over core).
Axes of the slice: x: 2, y: 2, z: 4, core: 2. Of those that a mesh axis runs over, the one named last changes fastest.
Arguments:
- constraint: bfloat16 [2048, 2, 64, 128], P(('grp', 'scen', 'bund')), parts along dimension 0, may hold values from -0.5 to 0.5
- demand: bfloat16 [2048, 2, 64], P(('grp', 'scen', 'bund')), parts along dimension 0, may hold values from -6 to 6
- start_duals: bfloat16 [2048, 2, 64], P(('grp', 'scen', 'bund')), parts along dimension 0, may hold values from -4 to 4
- unit_cost: bfloat16 [2048, 2, 128], P(('grp', 'scen', 'bund')), parts along dimension 0, may hold values from -4 to 4
- multiplier: bfloat16 [2048, 2, 128], P(('grp', 'scen', 'bund')), parts along dimension 0, may hold values from -4 to 4
- weight: bfloat16 [2048], P(('grp', 'scen', 'bund')), parts along dimension 0, may hold values from 0.25 to 4
- block_index: int32 [2048, 2], P(('grp', 'scen', 'bund')), parts along dimension 0, may hold values from 0 to 1023
- bundle_of: int32 [2048], P(('grp', 'scen', 'bund')), parts along dimension 0, may hold values from 0 to 15, as said below
- consensus: float32 [2097152], P(('grp', 'scen', 'bund')), parts along dimension 0, may hold values from 0 to 1
- capacity_limit: float32 [2097152], P(('grp', 'scen', 'bund')), parts along dimension 0, may hold values from 0.6 to 1.5
Outputs:
- consensus_new: float32 [2097152], P(('grp', 'scen', 'bund')), parts along dimension 0
- multiplier_new: float32 [2048, 2, 128], P(('grp', 'scen', 'bund')), parts along dimension 0
There are 2 independent parts, one for each index of `grp`. A program takes and returns all parts, laid end to end along the dimension named above; each array names one. Nothing has to cross between parts.
Inputs may be any that keep to these rules, and one draw needn't show every extreme that they name: `bundle_of`: at most 8 of the 64 scenarios of one device belong to one bundle; one bundle gets exactly 8 scenarios from every device.
All inputs are finite; a program needn't handle non-finite values.
Results may differ from a plain program's by a relative error of at most 0.0003.
Values may be sent and summed in bfloat16 or wider, within the bound.
A program may use at most 128 MiB of HBM per device.

v0:
```python
import jax
import jax.numpy as jnp
from jax import lax
from jax.sharding import PartitionSpec as P

penalty = 1.0
dual_step = 0.5
step_size = 0.5
anchor = 1.0


def shifted(block, axis, distance):
    devices = range(lax.axis_size(axis))
    route = [((i - distance) % len(devices), i) for i in devices]
    return lax.ppermute(block, axis, route)


def exact_einsum(pattern, left_side, right_side):
    return jnp.einsum(
        pattern,
        left_side,
        right_side,
        precision=lax.Precision.HIGHEST,
        preferred_element_type=jnp.float32,
    )


def body(
    constraint,
    demand,
    start_duals,
    unit_cost,
    multiplier,
    weight,
    block_index,
    bundle_of,
    consensus,
    capacity_limit,
):
    devices = lax.axis_size(("scen", "bund"))
    per_dev = constraint.shape[0]
    touched = constraint.shape[1]
    row_count = constraint.shape[2]
    block_cols = constraint.shape[3]
    capacity = max(2, (2 * per_dev + devices - 1) // devices)
    total_slots = devices * capacity
    share_blocks = consensus.shape[0] // block_cols
    region_len = 2 * share_blocks
    positions = jnp.arange(per_dev, dtype=jnp.int32)
    same_bundle = (bundle_of[:, None] == bundle_of[None, :]) & (
        positions[None, :] < positions[:, None]
    )
    order_in = jnp.sum(same_bundle.astype(jnp.int32), axis=1)
    target = bundle_of * capacity + order_in

    def place_rows(values):
        return jnp.zeros((total_slots,) + values.shape[1:], values.dtype).at[target].set(values)

    own_old = consensus.reshape(share_blocks, block_cols)
    own_limit = capacity_limit.reshape(share_blocks, block_cols)
    nearby = shifted(jnp.stack([own_old, own_limit]), ("scen", "bund"), -1)
    region_old = jnp.concatenate([own_old, nearby[0]], axis=0)
    region_high = jnp.concatenate([own_limit, nearby[1]], axis=0)
    packed = jnp.concatenate([demand, start_duals], axis=-1)
    vectors = jnp.stack([packed, unit_cost, multiplier], axis=1)
    outgoing = (
        place_rows(constraint),
        place_rows(vectors),
        place_rows(weight),
        place_rows(block_index),
    )
    arrived = (
        lax.all_to_all(outgoing[0], ("scen", "bund"), split_axis=0, concat_axis=0, tiled=True),
        lax.all_to_all(outgoing[1], ("scen", "bund"), split_axis=0, concat_axis=0, tiled=True),
        lax.all_to_all(outgoing[2], ("scen", "bund"), split_axis=0, concat_axis=0, tiled=True),
        lax.all_to_all(outgoing[3], ("scen", "bund"), split_axis=0, concat_axis=0, tiled=True),
    )
    matrices_in, vectors_in, weight_in, blocks_in = arrived
    targets = vectors_in[:, 0, :, :row_count].astype(jnp.float32)
    duals_zero = vectors_in[:, 0, :, row_count:].astype(jnp.float32)
    mult_in = vectors_in[:, 2].astype(jnp.float32)
    linear_terms = vectors_in[:, 1].astype(jnp.float32) + mult_in
    weights_in = weight_in.astype(jnp.float32)
    flat_blocks = blocks_in.reshape(-1)
    selector = (flat_blocks[:, None] == jnp.arange(region_len, dtype=jnp.int32)[None, :]).astype(
        jnp.float32
    )
    pair_weight = jnp.broadcast_to(weights_in[:, None], (total_slots, touched)).reshape(-1)
    totals = jnp.dot(pair_weight, selector, precision=lax.Precision.HIGHEST)

    def pick_rows(region):
        return jnp.take(region, flat_blocks, axis=0).reshape(total_slots, touched, block_cols)

    prior = pick_rows(region_old)

    def residual_of(current):
        return exact_einsum("skrc,skc->skr", matrices_in, pick_rows(current)) - targets

    def descend(current, inner_duals):
        local_cols = pick_rows(current)
        pulled = exact_einsum("skrc,skr->skc", matrices_in, inner_duals)
        slot_terms = weights_in[:, None, None] * (
            linear_terms + pulled + penalty * (local_cols - prior)
        )
        gradient = exact_einsum("ab,ac->bc", selector, slot_terms.reshape(-1, block_cols))
        return jnp.clip(current - step_size * gradient / (1.0 + totals)[:, None], 0.0, region_high)

    first_res = residual_of(region_old)
    zone_one = descend(region_old, duals_zero + dual_step * first_res)
    second_res = residual_of(zone_one)
    duals_next = duals_zero + dual_step * second_res
    zone_two = descend(zone_one, duals_next + dual_step * second_res)
    weighted = totals[:, None] * zone_two
    weight_cols = jnp.broadcast_to(totals[:, None], (region_len, block_cols))
    lower_half = jnp.stack([weighted[:share_blocks], weight_cols[:share_blocks]])
    upper_half = jnp.stack([weighted[share_blocks:], weight_cols[share_blocks:]])
    incoming = shifted(upper_half, ("scen", "bund"), 1)
    own_new = (anchor * own_old + (lower_half[0] + incoming[0])) / (
        anchor + (lower_half[1] + incoming[1])
    )
    next_new = shifted(own_new, ("scen", "bund"), -1)
    region_new = jnp.concatenate([own_new, next_new], axis=0)
    updated = mult_in + penalty * (pick_rows(zone_two) - pick_rows(region_new))
    returned = lax.all_to_all(updated, ("scen", "bund"), split_axis=0, concat_axis=0, tiled=True)
    multiplier_new = jnp.take(returned, target, axis=0)
    return (own_new.reshape(-1), multiplier_new)


def solution(mesh):
    return jax.shard_map(
        body,
        mesh=mesh,
        in_specs=(
            P(("grp", "scen", "bund"), None, None, None),
            P(("grp", "scen", "bund"), None, None),
            P(("grp", "scen", "bund"), None, None),
            P(("grp", "scen", "bund"), None, None),
            P(("grp", "scen", "bund"), None, None),
            P(("grp", "scen", "bund")),
            P(("grp", "scen", "bund"), None),
            P(("grp", "scen", "bund")),
            P(("grp", "scen", "bund")),
            P(("grp", "scen", "bund")),
        ),
        out_specs=(P(("grp", "scen", "bund")), P(("grp", "scen", "bund"), None, None)),
        check_vma=False,
    )
```

profile of v0, /device:TPU:0, one launch (start us, length us, event | category | flops | bytes accessed | tf_op | source)
XLA Modules:
  0.0 206.2 jit_solution(15397372419806826936)
XLA Ops:
  0.6 1.0 convert_reduce_fusion
  1.6 0.7 compare_and_fusion.1
  2.3 1.1 scatter_custom_fusion
  3.4 0.7 all_to_all.28
  4.1 7.4 %all-to-all-start = ((bf16[16,8,1]{1,2,0:T(2,128)(2,1)}), bf16[16,8,1]{1,2,0:T(2,128)(2,1)S(1)}, u32[]{:S(2)}, u32[]{:S(2)}) async-start(bf16[16,8,1]{1,2,0:T(2,128)(2,1)} %all_to_all.28), calls=%async_computation | async-start | bytes 16384 | tf_op jit(solution)/shard_map/all_to_all | solution.py:75
  11.5 0.8 copy.24
  12.3 0.8 scatter_custom_fusion.1
  13.0 0.8 copy.25
  13.8 4.0 %all-to-all-done = bf16[16,8,1]{1,2,0:T(2,128)(2,1)S(1)} async-done(((bf16[16,8,1]{1,2,0:T(2,128)(2,1)}), bf16[16,8,1]{1,2,0:T(2,128)(2,1)S(1)}, u32[]{:S(2)}, u32[]{:S(2)}) %all-to-all-start) | async-done | bytes 288 | tf_op jit(solution)/shard_map/all_to_all | solution.py:75
  17.8 3.5 %all-to-all-start.1 = ((s32[16,8,2]{1,2,0:T(2,128)}), s32[16,8,2]{1,2,0:T(2,128)S(1)}, u32[]{:S(2)}, u32[]{:S(2)}) async-start(s32[16,8,2]{1,2,0:T(2,128)} %copy.25), calls=%async_computation.1 | async-start | bytes 32768 | tf_op jit(solution)/shard_map/all_to_all | solution.py:76
  21.3 3.0 %broadcast_in_dim.33 = bf16[128,2,64,128]{3,2,1,0:T(8,128)(2,1)} broadcast(bf16[]{:T(256)} %constant.17.clone.1), dimensions={} | broadcast | bytes 4194306 | tf_op jit(solution)/shard_map/broadcast_in_dim | solution.py:57
  24.4 8.6 %scatter_fusion.1 = bf16[128,2,64,128]{3,2,1,0:T(8,128)(2,1)} fusion(bf16[128,2,64,128]{3,2,1,0:T(8,128)(2,1)} %broadcast_in_dim.33, s32[64]{0:T(128)S(1)} %get-tuple-element.4, bf16[64,2,64,128]{3,2,1,0:T(8,128)(2,1)S(1)} %copy-done.1), kind=kCustom, calls=%fused_computation.8 | custom fusion | bytes 6291712 | tf_op jit(solution)/shard_map/scatter | solution.py:57
  33.0 6.2 %all-to-all-start.3 = ((bf16[128,2,64,128]{3,2,1,0:T(8,128)(2,1)}), bf16[128,2,64,128]{3,2,1,0:T(8,128)(2,1)}, u32[]{:S(2)}, u32[]{:S(2)}) async-start(bf16[128,2,64,128]{3,2,1,0:T(8,128)(2,1)} %scatter_fusion.1), calls=%async_computation.3 | async-start | bytes 8388608 | tf_op jit(solution)/shard_map/all_to_all | solution.py:73
  39.3 4.4 %collective-permute-start = (f32[2,512,128]{2,1,0:T(8,128)S(1)}, f32[2,512,128]{2,1,0:T(8,128)S(1)}, u32[]{:S(2)}, u32[]{:S(2)}) collective-permute-start(f32[2,512,128]{2,1,0:T(8,128)S(1)} %pad_maximum_fusion), channel_id=1, source_target_pairs={{1,0},{2,1},{3,2},{4,3},{5,4},{6,5},{7,6},{8,7},{9,8},{10,9},{11,1... | collective-permute-start | bytes 1572872 | tf_op jit(solution)/shard_map/ppermute | solution.py:15
  43.8 0.2 pad_maximum_fusion.5
  44.1 0.8 broadcast_in_dim.32
  44.9 7.8 %scatter_fusion = bf16[128,3,2,128]{3,2,1,0:T(2,128)(2,1)} fusion(bf16[128,3,2,128]{3,2,1,0:T(2,128)(2,1)} %broadcast_in_dim.32, s32[64]{0:T(128)S(1)} %get-tuple-element.4, bf16[64,3,2,128]{3,2,1,0:T(2,128)(2,1)S(1)} %copy.27), kind=kCustom, calls=%fused_computation.7 | custom fusion | bytes 295168 | tf_op jit(solution)/shard_map/scatter | solution.py:57
  52.8 0.2 reshape.178
  53.0 0.2 copy.26
  53.2 0.1 eq.31
  53.3 0.5 fusion.8
  53.8 59.6 %collective-permute-done = f32[2,512,128]{2,1,0:T(8,128)S(1)} collective-permute-done((f32[2,512,128]{2,1,0:T(8,128)S(1)}, f32[2,512,128]{2,1,0:T(8,128)S(1)}, u32[]{:S(2)}, u32[]{:S(2)}) %collective-permute-start) | collective-permute-done | bytes 524320 | tf_op jit(solution)/shard_map/ppermute | solution.py:15
  113.5 0.7 gather_fusion.1
  114.2 2.7 %all-to-all-done.3 = bf16[128,2,64,128]{3,2,1,0:T(8,128)(2,1)} async-done(((bf16[128,2,64,128]{3,2,1,0:T(8,128)(2,1)}), bf16[128,2,64,128]{3,2,1,0:T(8,128)(2,1)}, u32[]{:S(2)}, u32[]{:S(2)}) %all-to-all-start.3) | async-done | bytes 4194336 | tf_op jit(solution)/shard_map/all_to_all | solution.py:73
  117.0 25.2 %all-to-all-start.2 = ((bf16[128,3,2,128]{3,2,1,0:T(2,128)(2,1)}), bf16[128,3,2,128]{3,2,1,0:T(2,128)(2,1)S(1)}, u32[]{:S(2)}, u32[]{:S(2)}) async-start(bf16[128,3,2,128]{3,2,1,0:T(2,128)(2,1)} %scatter_fusion), calls=%async_computation.2 | async-start | bytes 393216 | tf_op jit(solution)/shard_map/all_to_all | solution.py:74
  142.3 8.3 %fusion.25 = f32[128,2,1,64]{3,2,1,0:T(1,128)S(1)} fusion(bf16[128,2,64,128]{3,2,1,0:T(8,128)(2,1)} %all-to-all-done.3, f32[128,2,128,1]{2,3,1,0:T(1,128)S(1)} %bitcast.109), kind=kOutput, calls=%fused_computation.76 | convolution fusion | flops 25165824 | bytes 4390912 | tf_op jit(solution)/shard_map/skrc,skc->skr/dot_general | solution.py:19
  150.6 0.6 all-to-all-done.2
  151.2 0.1 convert_add_fusion.2
  151.3 5.1 %fusion.26 = f32[128,2,1,128]{3,2,1,0:T(1,128)S(1)} fusion(bf16[128,2,64,128]{3,2,1,0:T(8,128)(2,1)} %all-to-all-done.3, f32[128,2,64,1]{2,3,1,0:T(1,128)S(1)} %bitcast.123), kind=kOutput, calls=%fused_computation.77 | convolution fusion | flops 25165824 | bytes 4390912 | tf_op jit(solution)/shard_map/skrc,skr->skc/dot_general | solution.py:19
  156.4 0.2 add_multiply_fusion.1
  156.6 1.1 fusion.7
  157.7 0.7 gather_fusion.2
  158.6 8.3 %fusion.27 = f32[128,2,1,64]{3,2,1,0:T(1,128)S(1)} fusion(bf16[128,2,64,128]{3,2,1,0:T(8,128)(2,1)} %all-to-all-done.3, f32[128,2,128,1]{2,3,1,0:T(1,128)S(1)} %bitcast.114), kind=kOutput, calls=%fused_computation.78 | convolution fusion | flops 25165824 | bytes 4390912 | tf_op jit(solution)/shard_map/skrc,skc->skr/dot_general | solution.py:19
  166.9 0.2 add_add_fusion
  167.0 5.1 %fusion.28 = f32[128,2,1,128]{3,2,1,0:T(1,128)S(1)} fusion(bf16[128,2,64,128]{3,2,1,0:T(8,128)(2,1)} %all-to-all-done.3, f32[128,2,64,1]{2,3,1,0:T(1,128)S(1)} %bitcast.122), kind=kOutput, calls=%fused_computation.79 | convolution fusion | flops 25165824 | bytes 4390912 | tf_op jit(solution)/shard_map/skrc,skr->skc/dot_general | solution.py:19
  172.1 0.2 add_multiply_fusion
  172.3 1.2 broadcast_multiply_fusion
  173.6 0.1 stack.30
  173.8 11.3 %collective-permute-done.1 = f32[2,512,128]{2,1,0:T(8,128)S(1)} collective-permute-done((f32[2,512,128]{2,1,0:T(8,128)S(1)}, f32[2,512,128]{2,1,0:T(8,128)S(1)}, u32[]{:S(2)}, u32[]{:S(2)}) %collective-permute-start.1) | collective-permute-done | bytes 524320 | tf_op jit(solution)/shard_map/ppermute | solution.py:15
  185.1 0.2 fusion.14
  185.4 0.7 gather_fusion.3
  186.1 3.2 %collective-permute-done.2 = f32[512,128]{1,0:T(8,128)S(1)} collective-permute-done((f32[512,128]{1,0:T(8,128)S(1)}, f32[512,128]{1,0:T(8,128)S(1)}, u32[]{:S(2)}, u32[]{:S(2)}) %collective-permute-start.2) | collective-permute-done | bytes 262176 | tf_op jit(solution)/shard_map/ppermute | solution.py:15
  189.3 0.7 gather_fusion.4
  190.1 0.7 convert_add_fusion
  190.8 6.0 %all-to-all-start.4 = ((f32[128,2,128]{2,1,0:T(2,128)}), f32[128,2,128]{2,1,0:T(2,128)S(1)}, u32[]{:S(2)}, u32[]{:S(2)}) async-start(f32[128,2,128]{2,1,0:T(2,128)} %convert_add_fusion), calls=%async_computation.4 | async-start | bytes 262144 | tf_op jit(solution)/shard_map/all_to_all | solution.py:124
  196.8 7.9 %all-to-all-done.4 = f32[128,2,128]{2,1,0:T(2,128)S(1)} async-done(((f32[128,2,128]{2,1,0:T(2,128)}), f32[128,2,128]{2,1,0:T(2,128)S(1)}, u32[]{:S(2)}, u32[]{:S(2)}) %all-to-all-start.4) | async-done | bytes 131104 | tf_op jit(solution)/shard_map/all_to_all | solution.py:124
  204.8 0.7 gather_fusion
  205.4 0.8 broadcast_select_fusion.2
  (39 shorter events, 1.1 us)
Async XLA Ops:
  0.6 23.7 %copy-start.1 = (bf16[64,2,64,128]{3,2,1,0:T(8,128)(2,1)S(1)}, bf16[64,2,64,128]{3,2,1,0:T(8,128)(2,1)}, u32[]{:S(2)}) copy-start(bf16[64,2,64,128]{3,2,1,0:T(8,128)(2,1)} %param.12) | copy-start | bytes 6291460
  4.1 13.7 %all-to-all-start = ((bf16[16,8,1]{1,2,0:T(2,128)(2,1)}), bf16[16,8,1]{1,2,0:T(2,128)(2,1)S(1)}, u32[]{:S(2)}, u32[]{:S(2)}) async-start(bf16[16,8,1]{1,2,0:T(2,128)(2,1)} %all_to_all.28), calls=%async_computation | async-start | bytes 16384 | tf_op jit(solution)/shard_map/all_to_all | solution.py:75
  17.8 15.2 %all-to-all-start.1 = ((s32[16,8,2]{1,2,0:T(2,128)}), s32[16,8,2]{1,2,0:T(2,128)S(1)}, u32[]{:S(2)}, u32[]{:S(2)}) async-start(s32[16,8,2]{1,2,0:T(2,128)} %copy.25), calls=%async_computation.1 | async-start | bytes 32768 | tf_op jit(solution)/shard_map/all_to_all | solution.py:76
  33.0 6.3 %copy-start = (f32[65536]{0:T(1024)S(1)}, f32[65536]{0:T(1024)}, u32[]{:S(2)}) copy-start(f32[65536]{0:T(1024)} %param.20) | copy-start | bytes 786436
  33.0 6.3 %copy-start.3 = (f32[65536]{0:T(1024)S(1)}, f32[65536]{0:T(1024)}, u32[]{:S(2)}) copy-start(f32[65536]{0:T(1024)} %param.21) | copy-start | bytes 786436
  33.0 10.7 %copy-start.4 = (bf16[64,2,64]{2,1,0:T(2,128)(2,1)S(1)}, bf16[64,2,64]{2,1,0:T(2,128)(2,1)}, u32[]{:S(2)}) copy-start(bf16[64,2,64]{2,1,0:T(2,128)(2,1)} %param.14) | copy-start | bytes 49156
  33.0 10.7 %copy-start.5 = (bf16[64,2,64]{2,1,0:T(2,128)(2,1)S(1)}, bf16[64,2,64]{2,1,0:T(2,128)(2,1)}, u32[]{:S(2)}) copy-start(bf16[64,2,64]{2,1,0:T(2,128)(2,1)} %param.13) | copy-start | bytes 49156
  33.0 10.8 %copy-start.6 = (bf16[64,2,128]{2,1,0:T(2,128)(2,1)S(1)}, bf16[64,2,128]{2,1,0:T(2,128)(2,1)}, u32[]{:S(2)}) copy-start(bf16[64,2,128]{2,1,0:T(2,128)(2,1)} %param.16) | copy-start | bytes 98308
  33.0 10.8 %copy-start.7 = (bf16[64,2,128]{2,1,0:T(2,128)(2,1)S(1)}, bf16[64,2,128]{2,1,0:T(2,128)(2,1)}, u32[]{:S(2)}) copy-start(bf16[64,2,128]{2,1,0:T(2,128)(2,1)} %param.15) | copy-start | bytes 98308
  33.0 83.9 %all-to-all-start.3 = ((bf16[128,2,64,128]{3,2,1,0:T(8,128)(2,1)}), bf16[128,2,64,128]{3,2,1,0:T(8,128)(2,1)}, u32[]{:S(2)}, u32[]{:S(2)}) async-start(bf16[128,2,64,128]{3,2,1,0:T(8,128)(2,1)} %scatter_fusion.1), calls=%async_computation.3 | async-start | bytes 8388608 | tf_op jit(solution)/shard_map/all_to_all | solution.py:73
  39.3 74.1 %collective-permute-start = (f32[2,512,128]{2,1,0:T(8,128)S(1)}, f32[2,512,128]{2,1,0:T(8,128)S(1)}, u32[]{:S(2)}, u32[]{:S(2)}) collective-permute-start(f32[2,512,128]{2,1,0:T(8,128)S(1)} %pad_maximum_fusion), channel_id=1, source_target_pairs={{1,0},{2,1},{3,2},{4,3},{5,4},{6,5},{7,6},{8,7},{9,8},{10,9},{11,1... | collective-permute-start | bytes 1572872 | tf_op jit(solution)/shard_map/ppermute | solution.py:15
  117.0 34.2 %all-to-all-start.2 = ((bf16[128,3,2,128]{3,2,1,0:T(2,128)(2,1)}), bf16[128,3,2,128]{3,2,1,0:T(2,128)(2,1)S(1)}, u32[]{:S(2)}, u32[]{:S(2)}) async-start(bf16[128,3,2,128]{3,2,1,0:T(2,128)(2,1)} %scatter_fusion), calls=%async_computation.2 | async-start | bytes 393216 | tf_op jit(solution)/shard_map/all_to_all | solution.py:74
  173.8 11.4 %collective-permute-start.1 = (f32[2,512,128]{2,1,0:T(8,128)S(1)}, f32[2,512,128]{2,1,0:T(8,128)S(1)}, u32[]{:S(2)}, u32[]{:S(2)}) collective-permute-start(f32[2,512,128]{2,1,0:T(8,128)S(1)} %pad_maximum_fusion.3), channel_id=1, source_target_pairs={{15,0},{0,1},{1,2},{2,3},{3,4},{4,5},{5,6},{6,7},{7,8},{8,9},{9,10... | collective-permute-start | bytes 1572872 | tf_op jit(solution)/shard_map/ppermute | solution.py:15
  185.3 20.9 %copy-start.2 = (f32[512,128]{1,0:T(8,128)}, f32[512,128]{1,0:T(8,128)S(1)}, u32[]{:S(2)}) copy-start(f32[512,128]{1,0:T(8,128)S(1)} %fusion.14) | copy-start | bytes 786436
  185.3 3.9 %collective-permute-start.2 = (f32[512,128]{1,0:T(8,128)S(1)}, f32[512,128]{1,0:T(8,128)S(1)}, u32[]{:S(2)}, u32[]{:S(2)}) collective-permute-start(f32[512,128]{1,0:T(8,128)S(1)} %fusion.14), channel_id=1, source_target_pairs={{1,0},{2,1},{3,2},{4,3},{5,4},{6,5},{7,6},{8,7},{9,8},{10,9},{11,1... | collective-permute-start | bytes 786440 | tf_op jit(solution)/shard_map/ppermute | solution.py:15
  190.8 13.9 %all-to-all-start.4 = ((f32[128,2,128]{2,1,0:T(2,128)}), f32[128,2,128]{2,1,0:T(2,128)S(1)}, u32[]{:S(2)}, u32[]{:S(2)}) async-start(f32[128,2,128]{2,1,0:T(2,128)} %convert_add_fusion), calls=%async_computation.4 | async-start | bytes 262144 | tf_op jit(solution)/shard_map/all_to_all | solution.py:124
where the time goes:
time: 207 us; the launch traced here: 206 us
  waiting for transfers between devices  89.3 us (43%)
  starting transfers between devices  52.8 us (26%)
  matrix products  29.6 us (14%)
  local copies, waits for them, and re-layouts  28.8 us (14%)
  other arithmetic  4.8 us (2%)
    ppermute x3, waiting for transfers between devices, shifted(): return lax.ppermute(block, axis, route)  74 us
    dot_general x6, matrix products, exact_einsum(): jnp.einsum(pattern, left_side, right_side, precision=lax.Precision.HIGHES...  29.1 us
    all_to_all x1, starting transfers between devices, body(): lax.all_to_all(outgoing[1], ('scen', 'bund'), split_axis=0, concat_axis=0...  25.2 us
    scatter x4, local copies, waits for them, and re-layouts, place_rows(): jnp.zeros((total_slots,) + values.shape[1:], values.dtype).at[target]  18.2 us
    all_to_all x1, waiting for transfers between devices, body(): lax.all_to_all(updated, ('scen', 'bund'), split_axis=0, concat_axis=0, ti...  7.92 us
    all_to_all x1, starting transfers between devices, body(): lax.all_to_all(outgoing[2], ('scen', 'bund'), split_axis=0, concat_axis=0...  7.39 us
    all_to_all x1, starting transfers between devices, body(): lax.all_to_all(outgoing[0], ('scen', 'bund'), split_axis=0, concat_axis=0...  6.2 us
    all_to_all x1, starting transfers between devices, body(): lax.all_to_all(updated, ('scen', 'bund'), split_axis=0, concat_axis=0, ti...  5.98 us
  transfers between devices with their start and end apart: 8, of which 7 were waited for; matrix products, arithmetic and copies ran while one was open for 16% of the time, Pallas kernels for 0%

commit v1 on v0

v1 whole, which is shorter than its diff:
```python
import functools
import jax
import jax.numpy as jnp
from jax import lax
from jax.experimental import pallas as pl
from jax.experimental.pallas import tpu as pltpu
from jax.sharding import PartitionSpec as P

f32 = jnp.float32
bf16 = jnp.bfloat16
i32 = jnp.int32
CHUNK = 16


def split(x):
    hi = x.astype(bf16)
    lo = (x - hi.astype(f32)).astype(bf16)
    return jnp.concatenate([hi, lo], axis=1)


def mm(a, b):
    return jnp.dot(a, b, preferred_element_type=f32)


def mm_split(sel, x):
    out = mm(sel, split(x))
    c = x.shape[1]
    return out[:, :c] + out[:, c:]


def onehot(cond):
    return jnp.where(cond, 1.0, 0.0).astype(bf16)


def to_bytes(q):
    hi = lax.shift_right_logical(q, 8)
    lo = q & 255
    return jnp.concatenate([hi.astype(f32).astype(bf16), lo.astype(f32).astype(bf16)], axis=1)


def pack(q):
    half = q.shape[0] // 2
    return (q[:half] << 16) | q[half:]


def unpack(word):
    return jnp.concatenate([lax.shift_right_logical(word, 16), word & 65535], axis=0)


def kernel(
    n, n_bund, rh, sb, rb,
    meta_ref, lin_ref, base1_ref, base2_ref, a_ref, old_ref, high_ref,
    fresh_ref, diff_ref,
    meta_out, meta_in, rows_out, rows_in, scale_out, scale_in,
    e_ref, eq_ref, g_ref, gt_ref,
    send_sem, recv_sem, scale_send, scale_recv,
):
    me = lax.axis_index("scen") * n_bund + lax.axis_index("bund")
    pairs = meta_ref.shape[1]
    cols = old_ref.shape[1]
    half_slots = n * rh
    slots = 2 * half_slots

    def device(e):
        d = lax.rem(me + 1 + e, n)
        return {"scen": d // n_bund, "bund": lax.rem(d, n_bund)}

    barrier = pltpu.get_barrier_semaphore()

    def greet(e, c):
        pl.semaphore_signal(barrier, inc=1, device_id=device(e), device_id_type=pl.DeviceIdType.MESH)
        return c

    lax.fori_loop(0, n - 1, greet, 0)

    meta = meta_ref[...]
    meta_t = jnp.concatenate([meta] * (pairs // 8), axis=0).T
    bun_row, key_row, w_row = meta[0:1], meta[1:2], meta[2:3]
    bun_col, key_col, w_col = meta_t[:, 0:1], meta_t[:, 1:2], meta_t[:, 2:3]
    p_row = lax.broadcasted_iota(i32, (1, pairs), 1)
    p_col = lax.broadcasted_iota(i32, (pairs, 1), 0)
    same = bun_col == bun_row
    before = (p_row // 2) < (p_col // 2)
    after = (p_col // 2) < (p_row // 2)
    cnt_col = jnp.sum(jnp.where(same & before, 1.0, 0.0), axis=1, keepdims=True).astype(i32)
    cnt_row = jnp.sum(jnp.where(same & after, 1.0, 0.0), axis=0, keepdims=True).astype(i32)

    def code(bun, key, cnt, p):
        up = (key.astype(i32) >= sb).astype(i32)
        dest = bun.astype(i32) + up
        dest = jnp.where(dest >= n, dest - n, dest)
        entry = dest - me - 1
        entry = jnp.where(entry < 0, entry + n, entry)
        inner = cnt + (p & 1)
        return dest * (2 * rh) + up * rh + inner, up * half_slots + entry * rh + inner

    full_row, rel_row = code(bun_row, key_row, cnt_row, p_row)
    _, rel_col = code(bun_col, key_col, cnt_col, p_col)
    meta_out[...] = jnp.concatenate(
        [full_row.astype(f32), key_row, w_row, jnp.zeros((5, pairs), f32)], axis=0
    )
    pl.semaphore_wait(barrier, n - 1)

    def exchange_start(src_of, dst, ssem, rsem):
        def go(e, c):
            pltpu.make_async_remote_copy(
                src_ref=src_of(e), dst_ref=dst.at[n - 2 - e], send_sem=ssem, recv_sem=rsem,
                device_id=device(e), device_id_type=pl.DeviceIdType.MESH,
            ).start()
            return c
        lax.fori_loop(0, n - 1, go, 0)

    def wait_all(buf, sem):
        part = buf.at[pl.ds(0, n - 1)]
        pltpu.make_async_copy(part, part, sem).wait()

    exchange_start(lambda e: meta_out, meta_in, send_sem.at[0], recv_sem.at[0])
    meta_in[n - 1] = meta_out[...]
    g_ref[...] = onehot(rel_col == lax.broadcasted_iota(i32, (pairs, slots), 1))
    gt_ref[...] = onehot(rel_row == lax.broadcasted_iota(i32, (slots, pairs), 0))
    wait_all(meta_in, recv_sem.at[0])

    got = meta_in[...]
    code_in, key_in, w_in = got[:, 0:1, :], got[:, 1:2, :], got[:, 2:3, :]

    def slot_mask(h):
        want = me * (2 * rh) + h * rh + lax.broadcasted_iota(i32, (n, rh, pairs), 1)
        return code_in.astype(i32) == want

    masks = [slot_mask(0), slot_mask(1)]

    def slot_col(values):
        return jnp.concatenate(
            [
                jnp.sum(jnp.where(m, values, 0.0), axis=2, keepdims=True).reshape(half_slots, 1)
                for m in masks
            ],
            axis=0,
        )

    keys = slot_col(key_in + 1.0)
    w_slot = slot_col(w_in)
    up_slot = lax.broadcasted_iota(i32, (slots, 1), 0) >= half_slots
    local = jnp.where(up_slot, keys - sb, keys)
    local = jnp.where(keys > 0.0, local, 0.0)
    keys_row = jnp.broadcast_to(keys, (slots, 128)).T[0:1]
    local_row = jnp.broadcast_to(local, (slots, 128)).T[0:1]
    e_ref[...] = onehot(keys == keys_row)
    eq_ref[...] = onehot(local == local_row)
    own = onehot(local == lax.broadcasted_iota(i32, (slots, sb), 1).astype(f32) + 1.0)

    def send_rows(stage, codes):
        rows_out[stage] = pack(codes).reshape(n, rh, cols)
        exchange_start(
            lambda e: rows_out.at[stage, e], rows_in.at[stage], send_sem.at[stage + 1], recv_sem.at[stage + 1]
        )
        rows_in[stage, n - 1] = rows_out[stage, n - 1]

    def take_rows(stage):
        wait_all(rows_in.at[stage], recv_sem.at[stage + 1])
        return unpack(rows_in[stage].reshape(half_slots, cols))

    def zone_code(z):
        return jnp.minimum(jnp.round(z * 32768.0), 65535.0).astype(i32)

    prior = mm_split(own, old_ref[...])
    send_rows(0, zone_code(prior))
    high = mm_split(own, high_ref[...])
    w_wide = jnp.broadcast_to(w_slot, (slots, cols)).astype(bf16)
    totals = mm(e_ref[...], w_wide)
    step = 0.5 / (1.0 + totals)

    def home(stage, which, base_ref, dual):
        x = mm(g_ref[...], to_bytes(take_rows(stage))).astype(bf16)
        lanes = CHUNK * rb
        diag = lax.broadcasted_iota(i32, (CHUNK, lanes), 0) == (
            lax.broadcasted_iota(i32, (CHUNK, lanes), 1) // rb
        )
        pulled = []
        for c in range(pairs // CHUNK):
            a = a_ref[c * lanes:(c + 1) * lanes, :]
            xc = x[c * CHUNK:(c + 1) * CHUNK]
            xc = jnp.concatenate([xc[:, :cols], xc[:, cols:]], axis=0)
            r = lax.dot_general(xc, a, (((1,), (1,)), ((), ())), preferred_element_type=f32)
            r = (r[:CHUNK] * 256.0 + r[CHUNK:]) * (dual / 32768.0)
            inner = jnp.where(diag, r + base_ref[c:c + 1, :], 0.0)
            hi = inner.astype(bf16)
            lo = (inner - hi.astype(f32)).astype(bf16)
            g = mm(jnp.concatenate([hi, lo], axis=0), a)
            pulled.append(g[:CHUNK] + g[CHUNK:])
        terms = w_col * (lin_ref[...] + jnp.concatenate(pulled, axis=0))
        peak = jnp.maximum(jnp.max(jnp.abs(terms), axis=1, keepdims=True), 1e-30)
        unit = peak * (1.0 / 32767.0)
        scale_out[which] = jnp.broadcast_to(unit, (pairs, 128)).T[0:8]
        codes = jnp.round(terms / unit) + 32768.0
        codes = jnp.clip(codes, 0.0, 65535.0).astype(i32)
        exchange_start(lambda e: scale_out.at[which], scale_in.at[which], scale_send.at[which], scale_recv.at[which])
        scale_in[which, n - 1] = scale_out[which]
        placed = mm(gt_ref[...], to_bytes(codes))
        placed = (placed[:, :cols] * 256.0 + placed[:, cols:]).astype(i32)
        send_rows(stage + 1, placed)

    def gradient(stage, which):
        wait_all(scale_in.at[which], scale_recv.at[which])
        unit = slot_col(scale_in[which][:, 0:1, :])
        codes = take_rows(stage)
        terms = (codes - 32768).astype(f32) * unit
        return mm_split(e_ref[...], terms)

    home(0, 0, base1_ref, 0.5)
    zone_one = jnp.clip(prior - step * gradient(1, 0), 0.0, high)
    send_rows(2, zone_code(zone_one))
    home(2, 1, base2_ref, 1.0)
    grad = gradient(3, 1) + totals * (zone_one - prior)
    zone_two = jnp.clip(zone_one - step * grad, 0.0, high)
    weighted = w_slot * zone_two
    both = jnp.concatenate([split(weighted), w_wide], axis=1)
    sums = mm(eq_ref[...], both)
    fresh = (prior + (sums[:, :cols] + sums[:, cols:2 * cols])) / (1.0 + sums[:, 2 * cols:])
    delta = jnp.round((zone_two - fresh + 2.0) * 16384.0)
    send_rows(4, jnp.clip(delta, 0.0, 65535.0).astype(i32))
    own_t = onehot(local_row == lax.broadcasted_iota(i32, (sb, slots), 0).astype(f32) + 1.0)
    sums = mm(own_t, both)
    fresh_ref[...] = (old_ref[...] + (sums[:, :cols] + sums[:, cols:2 * cols])) / (
        1.0 + sums[:, 2 * cols:]
    )
    out = mm(g_ref[...], to_bytes(take_rows(4)))
    diff_ref[...] = (out[:, :cols] * 256.0 + out[:, cols:]) * (1.0 / 16384.0) - 2.0

    wait_all(meta_in, send_sem.at[0])
    for stage in range(5):
        wait_all(rows_in.at[stage], send_sem.at[stage + 1])
    for which in range(2):
        wait_all(scale_in.at[which], scale_send.at[which])


def body(
    constraint, demand, start_duals, unit_cost, multiplier, weight,
    block_index, bundle_of, consensus, capacity_limit,
):
    n = lax.axis_size(("scen", "bund"))
    n_bund = lax.axis_size("bund")
    per_dev, touched, rb, cols = constraint.shape
    pairs = per_dev * touched
    sb = consensus.shape[0] // cols
    capacity = max(2, (2 * per_dev + n - 1) // n)
    rh = -(-capacity * touched // 8) * 8
    half_slots = n * rh
    slots = 2 * half_slots

    wide = lambda v: jnp.broadcast_to(v.astype(f32)[:, None], (per_dev, touched)).reshape(1, pairs)
    meta = jnp.concatenate(
        [wide(bundle_of), block_index.astype(f32).reshape(1, pairs), wide(weight), jnp.zeros((5, pairs), f32)],
        axis=0,
    )
    mult = multiplier.astype(f32)
    lin = (unit_cost.astype(f32) + mult).reshape(pairs, cols)
    duals = start_duals.astype(f32)
    target = demand.astype(f32)
    lanes = CHUNK * rb
    base1 = (duals - 0.5 * target).reshape(pairs * rb // lanes, lanes)
    base2 = (duals - target).reshape(pairs * rb // lanes, lanes)

    vmem = pl.BlockSpec(memory_space=pltpu.VMEM)
    fresh, diff = pl.pallas_call(
        functools.partial(kernel, n, n_bund, rh, sb, rb),
        out_shape=(
            jax.ShapeDtypeStruct((sb, cols), f32),
            jax.ShapeDtypeStruct((pairs, cols), f32),
        ),
        in_specs=[vmem] * 7,
        out_specs=(vmem, vmem),
        scratch_shapes=[
            pltpu.VMEM((8, pairs), f32),
            pltpu.VMEM((n, 8, pairs), f32),
            pltpu.VMEM((5, n, rh, cols), i32),
            pltpu.VMEM((5, n, rh, cols), i32),
            pltpu.VMEM((2, 8, pairs), f32),
            pltpu.VMEM((2, n, 8, pairs), f32),
            pltpu.VMEM((slots, slots), bf16),
            pltpu.VMEM((slots, slots), bf16),
            pltpu.VMEM((pairs, slots), bf16),
            pltpu.VMEM((slots, pairs), bf16),
            pltpu.SemaphoreType.DMA((6,)),
            pltpu.SemaphoreType.DMA((6,)),
            pltpu.SemaphoreType.DMA((2,)),
            pltpu.SemaphoreType.DMA((2,)),
        ],
        compiler_params=pltpu.CompilerParams(
            collective_id=0, has_side_effects=True, vmem_limit_bytes=56 * 1024 * 1024
        ),
    )(
        meta, lin, base1, base2,
        constraint.reshape(pairs * rb, cols),
        consensus.reshape(sb, cols),
        capacity_limit.reshape(sb, cols),
    )
    return fresh.reshape(-1), mult + diff.reshape(per_dev, touched, cols)


def solution(mesh):
    split_all = ("grp", "scen", "bund")
    return jax.shard_map(
        body,
        mesh=mesh,
        in_specs=(
            P(split_all, None, None, None),
            P(split_all, None, None),
            P(split_all, None, None),
            P(split_all, None, None),
            P(split_all, None, None),
            P(split_all),
            P(split_all, None),
            P(split_all),
            P(split_all),
            P(split_all),
        ),
        out_specs=(P(split_all), P(split_all, None, None)),
        check_vma=False,
    )
```

time: 207 us -> 57.7 us (0.28)
  waiting for transfers between devices: 89.3 us -> 0 us
  starting transfers between devices: 52.8 us -> 0 us
  Pallas kernels: 0 us -> 46.3 us
  matrix products: 29.6 us -> 0 us
  local copies, waits for them, and re-layouts: 28.8 us -> 4.54 us
    ppermute x3 -> x0, waiting for transfers between devices: 74 us -> none  [shifted(): return lax.ppermute(block, axis, route)]
    all_to_all x5 -> x0, starting transfers between devices: 48.3 us -> none  [the longest x1 25.2 us: body(): lax.all_to_all(outgoing[1], ('scen', 'bund'), split_axis=0, concat_axis=0...]
    pallas_call x0 -> x1, Pallas kernels: none -> 46.3 us  [body(): pl.pallas_call(functools.partial(kernel, n, n_bund, rh, sb, rb), out_shap...]
    dot_general x7 -> x0, matrix products: 29.6 us -> none  [the longest x6 29.1 us: exact_einsum(): jnp.einsum(pattern, left_side, right_side, precision=lax.Precision.HIGHES...]
    scatter x4 -> x0, local copies, waits for them, and re-layouts: 18.2 us -> none  [place_rows(): jnp.zeros((total_slots,) + values.shape[1:], values.dtype).at[target]]
    all_to_all x5 -> x0, waiting for transfers between devices: 15.3 us -> none  [the longest x1 7.92 us: body(): lax.all_to_all(updated, ('scen', 'bund'), split_axis=0, concat_axis=0, ti...]
    ppermute x3 -> x0, starting transfers between devices: 4.5 us -> none  [shifted(): return lax.ppermute(block, axis, route)]
    gather x5 -> x0, local copies, waits for them, and re-layouts: 3.57 us -> none  [the longest x4 2.92 us: pick_rows(): jnp.take(region, flat_blocks, axis=0)]
  transfers between devices with their start and end apart: 8 -> 0, of which waited for: 7 -> 0; matrix products, arithmetic and copies ran while one was open for 16% -> 0% of each run, Pallas kernels for 0% -> 0%
where the time goes in v1:
time: 57.7 us; the launch traced here: 57.2 us
  Pallas kernels  46.3 us (80%)
  other arithmetic  5.72 us (10%)
  local copies, waits for them, and re-layouts  4.54 us (8%)
  between operations  0.67 us (1%)
    pallas_call x1, Pallas kernels, body(): pl.pallas_call(functools.partial(kernel, n, n_bund, rh, sb, rb), out_shap...  46.3 us
    unnamed x3, local copies, waits for them, and re-layouts  1.67 us
    add x1, other arithmetic, body(): return (fresh.reshape(-1), mult + diff.reshape(per_dev, touched, cols))  1.48 us
    add x1, other arithmetic, body(): lin = (unit_cost.astype(f32) + mult).reshape(pairs, cols)  1.41 us

profile of v1, /device:TPU:0, one launch (start us, length us, event | category | flops | bytes accessed | tf_op | source)
XLA Modules:
  0.0 57.2 jit_solution(581295679235077258)
XLA Ops:
  0.6 0.0 copy-start
  0.6 0.7 %convert_element_type.21 = f32[64]{0:T(128)S(1)} convert(s32[64]{0:T(128)} %param.17) | non-fusion elementwise | flops 64 | bytes 512 | tf_op jit(solution)/shard_map/convert_element_type | solution.py:251
  1.3 0.1 pad.3.clone
  1.4 0.7 %convert_element_type.22 = f32[64,2]{0,1:T(2,128)S(1)} convert(s32[64,2]{0,1:T(2,128)} %param.16) | non-fusion elementwise | flops 128 | bytes 1024 | tf_op jit(solution)/shard_map/convert_element_type | solution.py:253
  2.1 0.1 copy.13
  2.2 0.1 reshape.40
  2.3 0.1 broadcast_in_dim.6
  2.4 0.1 reshape.39
  2.5 0.7 %broadcast_in_dim.7 = f32[64,2]{1,0:T(8,128)S(1)} broadcast(bf16[64]{0:T(256)(128)(2,1)} %param.15), dimensions={0} | broadcast | bytes 640 | tf_op jit(solution)/shard_map/broadcast_in_dim | solution.py:251
  3.3 0.1 reshape.41
  3.4 0.7 %maximum_maximum_fusion.meta_ref = f32[8,128]{1,0:T(8,128)} fusion(f32[1,128]{1,0:T(1,128)S(1)} %reshape.41, f32[1,128]{1,0:T(1,128)S(1)} %reshape.40, f32[1,128]{1,0:T(1,128)S(1)} %reshape.39, f32[8]{0:T(128)S(1)} %pad.3.clone), kind=kLoop, calls=%fused_computation.5 | loop fusion | flops 3072 | bytes 5664 | tf_op jit(solution)/shard_map/concatenate | solution.py:252
  4.1 1.4 %convert_add_fusion.1 = f32[16,8,128]{2,1,0:T(8,128)} fusion(bf16[16,8,128]{2,1,0:T(8,128)(2,1)} %bitcast.17, bf16[16,8,128]{2,1,0:T(8,128)(2,1)} %bitcast.21), kind=kLoop, calls=%fused_computation.4 | loop fusion | flops 49152 | bytes 131072 | tf_op jit(solution)/shard_map/add | solution.py:257
  5.5 0.8 %convert_subtract_fusion = (f32[64,2,64]{2,1,0:T(2,128)S(1)}, f32[64,2,64]{2,1,0:T(2,128)S(1)}) fusion(bf16[64,2,64]{2,1,0:T(2,128)(2,1)} %param.11, bf16[64,2,64]{2,1,0:T(2,128)(2,1)} %param.12), kind=kLoop, calls=%fused_computation | loop fusion | flops 40960 | bytes 98304 | tf_op jit(solution)/shard_map/sub | solution.py:262
  6.3 0.7 %reshape.44.base2_ref = f32[8,1024]{1,0:T(8,128)} reshape(f32[64,2,64]{2,1,0:T(2,128)S(1)} %get-tuple-element.6) | data formatting | bytes 65536 | tf_op jit(solution)/shard_map/reshape | solution.py:262
  7.0 0.7 %reshape.43.base1_ref = f32[8,1024]{1,0:T(8,128)} reshape(f32[64,2,64]{2,1,0:T(2,128)S(1)} %get-tuple-element.7) | data formatting | bytes 65536 | tf_op jit(solution)/shard_map/reshape | solution.py:261
  7.8 46.3 %shard_map.113 = (f32[512,128]{1,0:T(8,128)}, f32[128,128]{1,0:T(8,128)}) custom-call(f32[8,128]{1,0:T(8,128)} %maximum_maximum_fusion.meta_ref, f32[128,128]{1,0:T(8,128)} %bitcast.13, f32[8,1024]{1,0:T(8,128)} %reshape.43.base1_ref, f32[8,1024]{1,0:T(8,128)} %reshape.44.base2_ref, bf16[8192,128]{1,0:T(8,128)(2,1)} %bitcast.12, f32[512,128]{1,0:T(8,128)} %bitcast.15, ...), custom_call_target="tpu_custom_call" | custom-call | tf_op jit(solution)/shard_map/pallas_call | solution.py:265
  54.1 0.0 copy-done
  54.1 1.5 %convert_add_fusion = f32[16,8,128]{2,1,0:T(8,128)} fusion(f32[16,8,128]{2,1,0:T(8,128)} %bitcast.20, bf16[16,8,128]{2,1,0:T(8,128)(2,1)S(1)} %bitcast.18), kind=kLoop, calls=%fused_computation.3 | loop fusion | flops 32768 | bytes 163840 | tf_op jit(solution)/shard_map/add | solution.py:298
  55.6 1.7 %copy.15 = f32[65536]{0:T(1024)} copy(f32[65536]{0:T(1024)} %bitcast.14) | data formatting | bytes 524288
  (1 shorter events, 0.0 us)
Async XLA Ops:
  0.6 53.4 %copy-start = (bf16[64,2,128]{2,1,0:T(2,128)(2,1)S(1)}, bf16[64,2,128]{2,1,0:T(2,128)(2,1)}, u32[]{:S(2)}) copy-start(bf16[64,2,128]{2,1,0:T(2,128)(2,1)} %param.14) | copy-start | bytes 98308

commit v2 on v1

--- a/solution.py
+++ b/solution.py
@@ -49,20 +49,27 @@
 
 def kernel(
     n, n_bund, rh, sb, rb,
-    meta_ref, lin_ref, base1_ref, base2_ref, a_ref, old_ref, high_ref,
-    fresh_ref, diff_ref,
+    bundle_ref, block_ref, weight_ref, unit_ref, mult_ref, dual_ref, demand_ref, a_hbm, old_ref, high_ref,
+    fresh_ref, out_ref,
     meta_out, meta_in, rows_out, rows_in, scale_out, scale_in,
-    e_ref, eq_ref, g_ref, gt_ref,
-    send_sem, recv_sem, scale_send, scale_recv,
+    e_ref, eq_ref, g_ref, gt_ref, own_ref, own_t_ref, a_ref, lin_ref, base_ref,
+    send_sem, recv_sem, scale_send, scale_recv, a_sem,
 ):
     me = lax.axis_index("scen") * n_bund + lax.axis_index("bund")
-    pairs = meta_ref.shape[1]
+    per_dev, touched = block_ref.shape
+    pairs = per_dev * touched
     cols = old_ref.shape[1]
     half_slots = n * rh
     slots = 2 * half_slots
 
+    bits = n.bit_length() - 1
+    mine = [lax.rem(me // (1 << b), 2) for b in range(bits)]
+
     def device(e):
-        d = lax.rem(me + 1 + e, n)
+        d = 0
+        for b in range(bits):
+            k = lax.rem((e + 1) // (1 << b), 2)
+            d = d + (mine[b] + k - 2 * mine[b] * k) * (1 << b)
         return {"scen": d // n_bund, "bund": lax.rem(d, n_bund)}
 
     barrier = pltpu.get_barrier_semaphore()
@@ -73,15 +80,22 @@
 
     lax.fori_loop(0, n - 1, greet, 0)
 
-    meta = meta_ref[...]
-    meta_t = jnp.concatenate([meta] * (pairs // 8), axis=0).T
-    bun_row, key_row, w_row = meta[0:1], meta[1:2], meta[2:3]
-    bun_col, key_col, w_col = meta_t[:, 0:1], meta_t[:, 1:2], meta_t[:, 2:3]
+    load_a = pltpu.make_async_copy(a_hbm, a_ref, a_sem)
+    load_a.start()
+
+    twice = lambda row: jnp.concatenate([row] * touched, axis=1)
+    bun_row = twice(bundle_ref[...].astype(f32))
+    w_row = twice(weight_ref[...].astype(f32))
+    key_col = jnp.concatenate([block_ref[:, j:j + 1] for j in range(touched)], axis=0).astype(f32)
+    rows = jnp.concatenate([bun_row, w_row, jnp.zeros((6, pairs), f32)], axis=0)
+    rows_t = jnp.concatenate([rows] * (pairs // 8), axis=0).T
+    bun_col, w_col = rows_t[:, 0:1], rows_t[:, 1:2]
+    key_row = jnp.broadcast_to(key_col, (pairs, 128)).T[0:1]
     p_row = lax.broadcasted_iota(i32, (1, pairs), 1)
     p_col = lax.broadcasted_iota(i32, (pairs, 1), 0)
     same = bun_col == bun_row
-    before = (p_row // 2) < (p_col // 2)
-    after = (p_col // 2) < (p_row // 2)
+    before = (p_row < per_dev) & (p_row < lax.rem(p_col, per_dev))
+    after = (p_col < per_dev) & (p_col < lax.rem(p_row, per_dev))
     cnt_col = jnp.sum(jnp.where(same & before, 1.0, 0.0), axis=1, keepdims=True).astype(i32)
     cnt_row = jnp.sum(jnp.where(same & after, 1.0, 0.0), axis=0, keepdims=True).astype(i32)
 
@@ -89,22 +103,20 @@
         up = (key.astype(i32) >= sb).astype(i32)
         dest = bun.astype(i32) + up
         dest = jnp.where(dest >= n, dest - n, dest)
-        entry = dest - me - 1
-        entry = jnp.where(entry < 0, entry + n, entry)
-        inner = cnt + (p & 1)
+        entry = jnp.where(dest == me, n, dest ^ me) - 1
+        inner = cnt * touched + p // per_dev
         return dest * (2 * rh) + up * rh + inner, up * half_slots + entry * rh + inner
 
     full_row, rel_row = code(bun_row, key_row, cnt_row, p_row)
     _, rel_col = code(bun_col, key_col, cnt_col, p_col)
-    meta_out[...] = jnp.concatenate(
-        [full_row.astype(f32), key_row, w_row, jnp.zeros((5, pairs), f32)], axis=0
-    )
+    meta_out[...] = jnp.concatenate([full_row.astype(f32), key_row, w_row], axis=1)
     pl.semaphore_wait(barrier, n - 1)
 
     def exchange_start(src_of, dst, ssem, rsem):
-        def go(e, c):
+        def go(k, c):
+            e = n - 2 - k
             pltpu.make_async_remote_copy(
-                src_ref=src_of(e), dst_ref=dst.at[n - 2 - e], send_sem=ssem, recv_sem=rsem,
+                src_ref=src_of(e), dst_ref=dst.at[e], send_sem=ssem, recv_sem=rsem,
                 device_id=device(e), device_id_type=pl.DeviceIdType.MESH,
             ).start()
             return c
@@ -121,7 +133,7 @@
     wait_all(meta_in, recv_sem.at[0])
 
     got = meta_in[...]
-    code_in, key_in, w_in = got[:, 0:1, :], got[:, 1:2, :], got[:, 2:3, :]
+    code_in, key_in, w_in = [got[:, :, i * pairs:(i + 1) * pairs] for i in range(3)]
 
     def slot_mask(h):
         want = me * (2 * rh) + h * rh + lax.broadcasted_iota(i32, (n, rh, pairs), 1)
@@ -145,9 +157,7 @@
     local = jnp.where(keys > 0.0, local, 0.0)
     keys_row = jnp.broadcast_to(keys, (slots, 128)).T[0:1]
     local_row = jnp.broadcast_to(local, (slots, 128)).T[0:1]
-    e_ref[...] = onehot(keys == keys_row)
-    eq_ref[...] = onehot(local == local_row)
-    own = onehot(local == lax.broadcasted_iota(i32, (slots, sb), 1).astype(f32) + 1.0)
+    own_ref[...] = onehot(local == lax.broadcasted_iota(i32, (slots, sb), 1).astype(f32) + 1.0)
 
     def send_rows(stage, codes):
         rows_out[stage] = pack(codes).reshape(n, rh, cols)
@@ -163,14 +173,24 @@
     def zone_code(z):
         return jnp.minimum(jnp.round(z * 32768.0), 65535.0).astype(i32)
 
-    prior = mm_split(own, old_ref[...])
+    prior = mm_split(own_ref[...], old_ref[...])
     send_rows(0, zone_code(prior))
-    high = mm_split(own, high_ref[...])
+    high = mm_split(own_ref[...], high_ref[...])
+    e_ref[...] = onehot(keys == keys_row)
     w_wide = jnp.broadcast_to(w_slot, (slots, cols)).astype(bf16)
     totals = mm(e_ref[...], w_wide)
     step = 0.5 / (1.0 + totals)
 
-    def home(stage, which, base_ref, dual):
+    for j in range(touched):
+        at = slice(j * per_dev, (j + 1) * per_dev)
+        lin_ref[at] = unit_ref[:, j, :].astype(f32) + mult_ref[:, j, :].astype(f32)
+        base_ref[0, at] = dual_ref[:, j, :].astype(f32)
+        base_ref[1, at] = demand_ref[:, j, :].astype(f32)
+    load_a.wait()
+
+    def home(stage, which, dual):
+        base = base_ref[0] - dual * base_ref[1]
+        base = jnp.concatenate([base] * (128 // rb), axis=1)
         x = mm(g_ref[...], to_bytes(take_rows(stage))).astype(bf16)
         lanes = CHUNK * rb
         diag = lax.broadcasted_iota(i32, (CHUNK, lanes), 0) == (
@@ -178,12 +198,15 @@
         )
         pulled = []
         for c in range(pairs // CHUNK):
-            a = a_ref[c * lanes:(c + 1) * lanes, :]
+            j, first = divmod(c * CHUNK, per_dev)
+            a = a_ref[first:first + CHUNK, j].reshape(lanes, cols)
+            bc = base[c * CHUNK:(c + 1) * CHUNK]
+            bc = jnp.concatenate([bc] * (lanes // 128), axis=1)
             xc = x[c * CHUNK:(c + 1) * CHUNK]
             xc = jnp.concatenate([xc[:, :cols], xc[:, cols:]], axis=0)
             r = lax.dot_general(xc, a, (((1,), (1,)), ((), ())), preferred_element_type=f32)
             r = (r[:CHUNK] * 256.0 + r[CHUNK:]) * (dual / 32768.0)
-            inner = jnp.where(diag, r + base_ref[c:c + 1, :], 0.0)
+            inner = jnp.where(diag, r + bc, 0.0)
             hi = inner.astype(bf16)
             lo = (inner - hi.astype(f32)).astype(bf16)
             g = mm(jnp.concatenate([hi, lo], axis=0), a)
@@ -191,7 +214,7 @@
         terms = w_col * (lin_ref[...] + jnp.concatenate(pulled, axis=0))
         peak = jnp.maximum(jnp.max(jnp.abs(terms), axis=1, keepdims=True), 1e-30)
         unit = peak * (1.0 / 32767.0)
-        scale_out[which] = jnp.broadcast_to(unit, (pairs, 128)).T[0:8]
+        scale_out[which] = jnp.broadcast_to(unit, (pairs, 128)).T[0:1]
         codes = jnp.round(terms / unit) + 32768.0
         codes = jnp.clip(codes, 0.0, 65535.0).astype(i32)
         exchange_start(lambda e: scale_out.at[which], scale_in.at[which], scale_send.at[which], scale_recv.at[which])
@@ -202,15 +225,17 @@
 
     def gradient(stage, which):
         wait_all(scale_in.at[which], scale_recv.at[which])
-        unit = slot_col(scale_in[which][:, 0:1, :])
+        unit = slot_col(scale_in[which])
         codes = take_rows(stage)
         terms = (codes - 32768).astype(f32) * unit
         return mm_split(e_ref[...], terms)
 
-    home(0, 0, base1_ref, 0.5)
+    home(0, 0, 0.5)
+    eq_ref[...] = onehot(local == local_row)
     zone_one = jnp.clip(prior - step * gradient(1, 0), 0.0, high)
     send_rows(2, zone_code(zone_one))
-    home(2, 1, base2_ref, 1.0)
+    home(2, 1, 1.0)
+    own_t_ref[...] = onehot(local_row == lax.broadcasted_iota(i32, (sb, slots), 0).astype(f32) + 1.0)
     grad = gradient(3, 1) + totals * (zone_one - prior)
     zone_two = jnp.clip(zone_one - step * grad, 0.0, high)
     weighted = w_slot * zone_two
@@ -219,13 +244,14 @@
     fresh = (prior + (sums[:, :cols] + sums[:, cols:2 * cols])) / (1.0 + sums[:, 2 * cols:])
     delta = jnp.round((zone_two - fresh + 2.0) * 16384.0)
     send_rows(4, jnp.clip(delta, 0.0, 65535.0).astype(i32))
-    own_t = onehot(local_row == lax.broadcasted_iota(i32, (sb, slots), 0).astype(f32) + 1.0)
-    sums = mm(own_t, both)
+    sums = mm(own_t_ref[...], both)
     fresh_ref[...] = (old_ref[...] + (sums[:, :cols] + sums[:, cols:2 * cols])) / (
         1.0 + sums[:, 2 * cols:]
     )
     out = mm(g_ref[...], to_bytes(take_rows(4)))
-    diff_ref[...] = (out[:, :cols] * 256.0 + out[:, cols:]) * (1.0 / 16384.0) - 2.0
+    diff = (out[:, :cols] * 256.0 + out[:, cols:]) * (1.0 / 16384.0) - 2.0
+    for j in range(touched):
+        out_ref[:, j, :] = mult_ref[:, j, :].astype(f32) + diff[j * per_dev:(j + 1) * per_dev]
 
     wait_all(meta_in, send_sem.at[0])
     for stage in range(5):
@@ -248,54 +274,49 @@
     half_slots = n * rh
     slots = 2 * half_slots
 
-    wide = lambda v: jnp.broadcast_to(v.astype(f32)[:, None], (per_dev, touched)).reshape(1, pairs)
-    meta = jnp.concatenate(
-        [wide(bundle_of), block_index.astype(f32).reshape(1, pairs), wide(weight), jnp.zeros((5, pairs), f32)],
-        axis=0,
-    )
-    mult = multiplier.astype(f32)
-    lin = (unit_cost.astype(f32) + mult).reshape(pairs, cols)
-    duals = start_duals.astype(f32)
-    target = demand.astype(f32)
-    lanes = CHUNK * rb
-    base1 = (duals - 0.5 * target).reshape(pairs * rb // lanes, lanes)
-    base2 = (duals - target).reshape(pairs * rb // lanes, lanes)
-
     vmem = pl.BlockSpec(memory_space=pltpu.VMEM)
-    fresh, diff = pl.pallas_call(
+    fresh, updated = pl.pallas_call(
         functools.partial(kernel, n, n_bund, rh, sb, rb),
         out_shape=(
             jax.ShapeDtypeStruct((sb, cols), f32),
-            jax.ShapeDtypeStruct((pairs, cols), f32),
+            jax.ShapeDtypeStruct((per_dev, touched, cols), f32),
         ),
-        in_specs=[vmem] * 7,
+        in_specs=[vmem] * 7 + [pl.BlockSpec(memory_space=pl.ANY)] + [vmem] * 2,
         out_specs=(vmem, vmem),
         scratch_shapes=[
-            pltpu.VMEM((8, pairs), f32),
-            pltpu.VMEM((n, 8, pairs), f32),
+            pltpu.VMEM((1, 3 * pairs), f32),
+            pltpu.VMEM((n, 1, 3 * pairs), f32),
             pltpu.VMEM((5, n, rh, cols), i32),
             pltpu.VMEM((5, n, rh, cols), i32),
-            pltpu.VMEM((2, 8, pairs), f32),
-            pltpu.VMEM((2, n, 8, pairs), f32),
+            pltpu.VMEM((2, 1, pairs), f32),
+            pltpu.VMEM((2, n, 1, pairs), f32),
             pltpu.VMEM((slots, slots), bf16),
             pltpu.VMEM((slots, slots), bf16),
             pltpu.VMEM((pairs, slots), bf16),
             pltpu.VMEM((slots, pairs), bf16),
+            pltpu.VMEM((slots, sb), bf16),
+            pltpu.VMEM((sb, slots), bf16),
+            pltpu.VMEM(constraint.shape, bf16),
+            pltpu.VMEM((pairs, cols), f32),
+            pltpu.VMEM((2, pairs, rb), f32),
             pltpu.SemaphoreType.DMA((6,)),
             pltpu.SemaphoreType.DMA((6,)),
             pltpu.SemaphoreType.DMA((2,)),
             pltpu.SemaphoreType.DMA((2,)),
+            pltpu.SemaphoreType.DMA,
         ],
         compiler_params=pltpu.CompilerParams(
             collective_id=0, has_side_effects=True, vmem_limit_bytes=56 * 1024 * 1024
         ),
     )(
-        meta, lin, base1, base2,
-        constraint.reshape(pairs * rb, cols),
+        bundle_of.reshape(1, per_dev),
+        block_index,
+        weight.reshape(1, per_dev),
+        unit_cost, multiplier, start_duals, demand, constraint,
         consensus.reshape(sb, cols),
         capacity_limit.reshape(sb, cols),
     )
-    return fresh.reshape(-1), mult + diff.reshape(per_dev, touched, cols)
+    return fresh.reshape(-1), updated
 
 
 def solution(mesh):

time: 57.7 us -> 49.3 us (0.85)
  other arithmetic: 5.72 us -> 0 us
  Pallas kernels: 46.3 us -> 43.9 us
    add x2 -> x0, other arithmetic: 2.89 us -> none  [the longest x1 1.48 us: body(): return (fresh.reshape(-1), mult + diff.reshape(per_dev, touched, cols))]
    unnamed x3, local copies, waits for them, and re-layouts: 1.67 us -> 4.52 us
    pallas_call x1, Pallas kernels: 46.3 us -> 43.9 us  [body(): pl.pallas_call(functools.partial(kernel, n, n_bund, rh, sb, rb), out_shap...]
    reshape x5 -> x0, local copies, waits for them, and re-layouts: 1.89 us -> none  [the longest x1 0.74 us: body(): base1 = (duals - 0.5 * target).reshape(pairs * rb // lanes, lanes)]
    convert_element_type x2 -> x0, other arithmetic: 1.34 us -> none  [the longest x1 0.68 us: body(): block_index.astype(f32).reshape(1, pairs)]
    sub x1 -> x0, other arithmetic: 0.83 us -> none  [body(): base2 = (duals - target).reshape(pairs * rb // lanes, lanes)]
    broadcast_in_dim x3 -> x0, local copies, waits for them, and re-layouts: 0.8 us -> none  [the longest x2 0.8 us: body(): jnp.broadcast_to(v.astype(f32)[:, None], (per_dev, touched))]
    concatenate x1 -> x0, other arithmetic: 0.66 us -> none  [body(): jnp.concatenate([wide(bundle_of), block_index.astype(f32).reshape(1, pair...]
where the time goes in v2:
time: 49.3 us; the launch traced here: 49 us
  Pallas kernels  43.9 us (89%)
  local copies, waits for them, and re-layouts  4.52 us (9%)
  between operations  0.64 us (1%)
    pallas_call x1, Pallas kernels, body(): pl.pallas_call(functools.partial(kernel, n, n_bund, rh, sb, rb), out_shap...  43.9 us
    unnamed x3, local copies, waits for them, and re-layouts  4.52 us

profile of v2, /device:TPU:0, one launch (start us, length us, event | category | flops | bytes accessed | tf_op | source)
XLA Modules:
  0.0 49.0 jit_solution(7343758700721664534)
XLA Ops:
  0.6 1.4 %copy.12.block_ref = s32[64,2]{1,0:T(8,128)} copy(s32[64,2]{0,1:T(2,128)} %param.16) | data formatting | bytes 1024 | tf_op args[6]
  2.0 43.9 %shard_map.113 = (f32[512,128]{1,0:T(8,128)}, f32[64,2,128]{2,1,0:T(2,128)}) custom-call(s32[1,64]{1,0:T(1,128)} %bitcast.8, s32[64,2]{1,0:T(8,128)} %copy.12.block_ref, bf16[1,64]{1,0:T(2,128)(2,1)} %bitcast.9, bf16[64,2,128]{2,1,0:T(2,128)(2,1)} %unit_ref.1, bf16[64,2,128]{2,1,0:T(2,128)(2,1)} %mult_ref.1, bf16[64,2,64]{2,1,0:T(2,128)(2,1)} %dual_ref.1, ...), custom_call_target="tpu_custom_call" | custom-call | tf_op jit(solution)/shard_map/pallas_call | solution.py:278
  45.9 1.7 %copy.15 = f32[65536]{0:T(1024)} copy(f32[65536]{0:T(1024)} %bitcast.7) | data formatting | bytes 524288
  47.5 1.5 %copy.16 = f32[64,2,128]{2,1,0:T(2,128)} copy(f32[64,2,128]{2,1,0:T(2,128)} %get-tuple-element.9) | data formatting | bytes 131072

commit v3 on v2

--- a/solution.py
+++ b/solution.py
@@ -49,16 +49,16 @@
 
 def kernel(
     n, n_bund, rh, sb, rb,
-    bundle_ref, block_ref, weight_ref, unit_ref, mult_ref, dual_ref, demand_ref, a_hbm, old_ref, high_ref,
+    bundle_ref, block_ref, weight_ref, unit_ref, mult_ref, dual_ref, demand_ref, a_hbm, old_hbm, high_hbm,
     fresh_ref, out_ref,
     meta_out, meta_in, rows_out, rows_in, scale_out, scale_in,
-    e_ref, eq_ref, g_ref, gt_ref, own_ref, own_t_ref, a_ref, lin_ref, base_ref,
-    send_sem, recv_sem, scale_send, scale_recv, a_sem,
+    e_ref, eq_ref, g_ref, gt_ref, own_ref, own_t_ref, a_ref, lin_ref, base_ref, old_ref, high_ref,
+    send_sem, recv_sem, scale_send, scale_recv, load_sem,
 ):
     me = lax.axis_index("scen") * n_bund + lax.axis_index("bund")
-    per_dev, touched = block_ref.shape
+    touched, per_dev = block_ref.shape
     pairs = per_dev * touched
-    cols = old_ref.shape[1]
+    cols = old_hbm.shape[1]
     half_slots = n * rh
     slots = 2 * half_slots
 
@@ -78,19 +78,22 @@
         pl.semaphore_signal(barrier, inc=1, device_id=device(e), device_id_type=pl.DeviceIdType.MESH)
         return c
 
-    lax.fori_loop(0, n - 1, greet, 0)
-
-    load_a = pltpu.make_async_copy(a_hbm, a_ref, a_sem)
-    load_a.start()
+    lax.fori_loop(0, n - 1, greet, 0, unroll=n <= 16)
+
+    loads = [
+        pltpu.make_async_copy(src, dst, load_sem.at[i])
+        for i, (src, dst) in enumerate([(old_hbm, old_ref), (high_hbm, high_ref), (a_hbm, a_ref)])
+    ]
+    for load in loads:
+        load.start()
 
     twice = lambda row: jnp.concatenate([row] * touched, axis=1)
     bun_row = twice(bundle_ref[...].astype(f32))
     w_row = twice(weight_ref[...].astype(f32))
-    key_col = jnp.concatenate([block_ref[:, j:j + 1] for j in range(touched)], axis=0).astype(f32)
-    rows = jnp.concatenate([bun_row, w_row, jnp.zeros((6, pairs), f32)], axis=0)
+    key_row = jnp.concatenate([block_ref[j:j + 1] for j in range(touched)], axis=1).astype(f32)
+    rows = jnp.concatenate([bun_row, w_row, key_row, jnp.zeros((5, pairs), f32)], axis=0)
     rows_t = jnp.concatenate([rows] * (pairs // 8), axis=0).T
-    bun_col, w_col = rows_t[:, 0:1], rows_t[:, 1:2]
-    key_row = jnp.broadcast_to(key_col, (pairs, 128)).T[0:1]
+    bun_col, w_col, key_col = rows_t[:, 0:1], rows_t[:, 1:2], rows_t[:, 2:3]
     p_row = lax.broadcasted_iota(i32, (1, pairs), 1)
     p_col = lax.broadcasted_iota(i32, (pairs, 1), 0)
     same = bun_col == bun_row
@@ -120,7 +123,7 @@
                 device_id=device(e), device_id_type=pl.DeviceIdType.MESH,
             ).start()
             return c
-        lax.fori_loop(0, n - 1, go, 0)
+        lax.fori_loop(0, n - 1, go, 0, unroll=n <= 16)
 
     def wait_all(buf, sem):
         part = buf.at[pl.ds(0, n - 1)]
@@ -173,8 +176,10 @@
     def zone_code(z):
         return jnp.minimum(jnp.round(z * 32768.0), 65535.0).astype(i32)
 
+    loads[0].wait()
     prior = mm_split(own_ref[...], old_ref[...])
     send_rows(0, zone_code(prior))
+    loads[1].wait()
     high = mm_split(own_ref[...], high_ref[...])
     e_ref[...] = onehot(keys == keys_row)
     w_wide = jnp.broadcast_to(w_slot, (slots, cols)).astype(bf16)
@@ -186,7 +191,7 @@
         lin_ref[at] = unit_ref[:, j, :].astype(f32) + mult_ref[:, j, :].astype(f32)
         base_ref[0, at] = dual_ref[:, j, :].astype(f32)
         base_ref[1, at] = demand_ref[:, j, :].astype(f32)
-    load_a.wait()
+    loads[2].wait()
 
     def home(stage, which, dual):
         base = base_ref[0] - dual * base_ref[1]
@@ -260,6 +265,17 @@
         wait_all(scale_in.at[which], scale_send.at[which])
 
 
+def hand_on(fresh_in, updated_in, fresh_ref, updated_ref, sem):
+    copies = [
+        pltpu.make_async_copy(fresh_in, fresh_ref, sem.at[0]),
+        pltpu.make_async_copy(updated_in, updated_ref, sem.at[1]),
+    ]
+    for copy in copies:
+        copy.start()
+    for copy in copies:
+        copy.wait()
+
+
 def body(
     constraint, demand, start_duals, unit_cost, multiplier, weight,
     block_index, bundle_of, consensus, capacity_limit,
@@ -275,13 +291,14 @@
     slots = 2 * half_slots
 
     vmem = pl.BlockSpec(memory_space=pltpu.VMEM)
+    anywhere = pl.BlockSpec(memory_space=pl.ANY)
     fresh, updated = pl.pallas_call(
         functools.partial(kernel, n, n_bund, rh, sb, rb),
         out_shape=(
             jax.ShapeDtypeStruct((sb, cols), f32),
             jax.ShapeDtypeStruct((per_dev, touched, cols), f32),
         ),
-        in_specs=[vmem] * 7 + [pl.BlockSpec(memory_space=pl.ANY)] + [vmem] * 2,
+        in_specs=[vmem] * 7 + [anywhere] * 3,
         out_specs=(vmem, vmem),
         scratch_shapes=[
             pltpu.VMEM((1, 3 * pairs), f32),
@@ -299,23 +316,35 @@
             pltpu.VMEM(constraint.shape, bf16),
             pltpu.VMEM((pairs, cols), f32),
             pltpu.VMEM((2, pairs, rb), f32),
+            pltpu.VMEM((sb, cols), f32),
+            pltpu.VMEM((sb, cols), f32),
             pltpu.SemaphoreType.DMA((6,)),
             pltpu.SemaphoreType.DMA((6,)),
             pltpu.SemaphoreType.DMA((2,)),
             pltpu.SemaphoreType.DMA((2,)),
-            pltpu.SemaphoreType.DMA,
+            pltpu.SemaphoreType.DMA((3,)),
         ],
         compiler_params=pltpu.CompilerParams(
             collective_id=0, has_side_effects=True, vmem_limit_bytes=56 * 1024 * 1024
         ),
     )(
         bundle_of.reshape(1, per_dev),
-        block_index,
+        block_index.T,
         weight.reshape(1, per_dev),
         unit_cost, multiplier, start_duals, demand, constraint,
         consensus.reshape(sb, cols),
         capacity_limit.reshape(sb, cols),
     )
+    fresh, updated = pl.pallas_call(
+        hand_on,
+        out_shape=(
+            jax.ShapeDtypeStruct(fresh.shape, f32),
+            jax.ShapeDtypeStruct(updated.shape, f32),
+        ),
+        in_specs=[vmem] * 2,
+        out_specs=(anywhere, anywhere),
+        scratch_shapes=[pltpu.SemaphoreType.DMA((2,))],
+    )(fresh, updated)
     return fresh.reshape(-1), updated
 
 

time: 49.3 us -> 45.3 us (0.919)
  local copies, waits for them, and re-layouts: 4.52 us -> 0 us
  Pallas kernels: 43.9 us -> 44.5 us
    unnamed x3 -> x0, local copies, waits for them, and re-layouts: 4.52 us -> none
    pallas_call x0 -> x1, Pallas kernels: none -> 1.68 us  [body(): pl.pallas_call(hand_on, out_shape=(jax.ShapeDtypeStruct(fresh.shape, f32)...]
    pallas_call x1, Pallas kernels: 43.9 us -> 42.8 us  [body(): pl.pallas_call(functools.partial(kernel, n, n_bund, rh, sb, rb), out_shap...]
where the time goes in v3:
time: 45.3 us; the launch traced here: 45.1 us
  Pallas kernels  44.5 us (98%)
  between operations  0.64 us (1%)
    pallas_call x1, Pallas kernels, body(): pl.pallas_call(functools.partial(kernel, n, n_bund, rh, sb, rb), out_shap...  42.8 us
    pallas_call x1, Pallas kernels, body(): pl.pallas_call(hand_on, out_shape=(jax.ShapeDtypeStruct(fresh.shape, f32)...  1.68 us

profile of v3, /device:TPU:0, one launch (start us, length us, event | category | flops | bytes accessed | tf_op | source)
XLA Modules:
  0.0 45.1 jit_solution(6858169414794291568)
XLA Ops:
  0.6 42.8 %shard_map.113 = (f32[512,128]{1,0:T(8,128)}, f32[64,2,128]{2,1,0:T(2,128)}) custom-call(s32[1,64]{1,0:T(1,128)} %bitcast.9, s32[2,64]{1,0:T(2,128)} %bitcast.8, bf16[1,64]{1,0:T(2,128)(2,1)} %bitcast.10, bf16[64,2,128]{2,1,0:T(2,128)(2,1)} %unit_ref.1, bf16[64,2,128]{2,1,0:T(2,128)(2,1)} %mult_ref.1, bf16[64,2,64]{2,1,0:T(2,128)(2,1)} %dual_ref.1, ...), custom_call_target="tpu_custom_call" | custom-call | tf_op jit(solution)/shard_map/pallas_call | solution.py:295
  43.4 1.7 %shard_map.114 = (f32[512,128]{1,0:T(8,128)}, f32[64,2,128]{2,1,0:T(2,128)}) custom-call(f32[512,128]{1,0:T(8,128)} %get-tuple-element.6.fresh_in, f32[64,2,128]{2,1,0:T(2,128)} %get-tuple-element.7.updated_in), custom_call_target="tpu_custom_call" | custom-call | tf_op jit(solution)/shard_map/pallas_call | solution.py:338

commit v4 on v3

--- a/solution.py
+++ b/solution.py
@@ -52,7 +52,7 @@
     bundle_ref, block_ref, weight_ref, unit_ref, mult_ref, dual_ref, demand_ref, a_hbm, old_hbm, high_hbm,
     fresh_ref, out_ref,
     meta_out, meta_in, rows_out, rows_in, scale_out, scale_in,
-    e_ref, eq_ref, g_ref, gt_ref, own_ref, own_t_ref, a_ref, lin_ref, base_ref, old_ref, high_ref,
+    e_ref, eq_ref, g_ref, gt_ref, own_ref, own_t_ref, a_ref, wide_ref, wide_t_ref, lin_ref, base_ref, old_ref, high_ref,
     send_sem, recv_sem, scale_send, scale_recv, load_sem,
 ):
     me = lax.axis_index("scen") * n_bund + lax.axis_index("bund")
@@ -61,14 +61,17 @@
     cols = old_hbm.shape[1]
     half_slots = n * rh
     slots = 2 * half_slots
+    near = n // 2
+    group_slots = slots // 2
+    groups = [slice(0, group_slots), slice(group_slots, slots)]
 
     bits = n.bit_length() - 1
     mine = [lax.rem(me // (1 << b), 2) for b in range(bits)]
 
-    def device(e):
+    def device(x):
         d = 0
         for b in range(bits):
-            k = lax.rem((e + 1) // (1 << b), 2)
+            k = lax.rem(x // (1 << b), 2)
             d = d + (mine[b] + k - 2 * mine[b] * k) * (1 << b)
         return {"scen": d // n_bund, "bund": lax.rem(d, n_bund)}
 
@@ -78,7 +81,7 @@
         pl.semaphore_signal(barrier, inc=1, device_id=device(e), device_id_type=pl.DeviceIdType.MESH)
         return c
 
-    lax.fori_loop(0, n - 1, greet, 0, unroll=n <= 16)
+    lax.fori_loop(1, n, greet, 0, unroll=n <= 16)
 
     loads = [
         pltpu.make_async_copy(src, dst, load_sem.at[i])
@@ -106,163 +109,213 @@
         up = (key.astype(i32) >= sb).astype(i32)
         dest = bun.astype(i32) + up
         dest = jnp.where(dest >= n, dest - n, dest)
-        entry = jnp.where(dest == me, n, dest ^ me) - 1
+        entry = dest ^ me
+        far = (entry >= near).astype(i32)
         inner = cnt * touched + p // per_dev
-        return dest * (2 * rh) + up * rh + inner, up * half_slots + entry * rh + inner
+        slot = far * group_slots + up * (near * rh) + (entry - far * near) * rh + inner
+        return dest * (2 * rh) + up * rh + inner, slot
 
     full_row, rel_row = code(bun_row, key_row, cnt_row, p_row)
     _, rel_col = code(bun_col, key_col, cnt_col, p_col)
     meta_out[...] = jnp.concatenate([full_row.astype(f32), key_row, w_row], axis=1)
     pl.semaphore_wait(barrier, n - 1)
 
-    def exchange_start(src_of, dst, ssem, rsem):
+    def send_group(g, messages):
+        first, last = (1, near) if g == 0 else (near, n)
+
         def go(k, c):
-            e = n - 2 - k
-            pltpu.make_async_remote_copy(
-                src_ref=src_of(e), dst_ref=dst.at[e], send_sem=ssem, recv_sem=rsem,
-                device_id=device(e), device_id_type=pl.DeviceIdType.MESH,
-            ).start()
+            x = first + last - 1 - k
+            for src_of, dst, ssem, rsem in messages:
+                pltpu.make_async_remote_copy(
+                    src_ref=src_of(x), dst_ref=dst.at[x], send_sem=ssem, recv_sem=rsem.at[g],
+                    device_id=device(x), device_id_type=pl.DeviceIdType.MESH,
+                ).start()
             return c
-        lax.fori_loop(0, n - 1, go, 0, unroll=n <= 16)
-
-    def wait_all(buf, sem):
-        part = buf.at[pl.ds(0, n - 1)]
+        lax.fori_loop(first, last, go, 0, unroll=n <= 16)
+
+    def wait_part(buf, first, last, sem):
+        part = buf.at[pl.ds(first, last - first)]
         pltpu.make_async_copy(part, part, sem).wait()
 
-    exchange_start(lambda e: meta_out, meta_in, send_sem.at[0], recv_sem.at[0])
-    meta_in[n - 1] = meta_out[...]
+    def wait_group(g, buf, sem):
+        first, last = (1, near) if g == 0 else (near, n)
+        wait_part(buf, first, last, sem.at[g])
+
+    def wait_sent(buf, sem):
+        wait_part(buf, 1, n, sem)
+
+    for g in (1, 0):
+        send_group(g, [(lambda x: meta_out, meta_in, send_sem.at[0], recv_sem.at[0])])
+    meta_in[0] = meta_out[...]
     g_ref[...] = onehot(rel_col == lax.broadcasted_iota(i32, (pairs, slots), 1))
     gt_ref[...] = onehot(rel_row == lax.broadcasted_iota(i32, (slots, pairs), 0))
-    wait_all(meta_in, recv_sem.at[0])
-
-    got = meta_in[...]
-    code_in, key_in, w_in = [got[:, :, i * pairs:(i + 1) * pairs] for i in range(3)]
-
-    def slot_mask(h):
-        want = me * (2 * rh) + h * rh + lax.broadcasted_iota(i32, (n, rh, pairs), 1)
-        return code_in.astype(i32) == want
-
-    masks = [slot_mask(0), slot_mask(1)]
-
-    def slot_col(values):
+
+    lanes = CHUNK * rb
+    loads[2].wait()
+    for c in range(pairs // (2 * CHUNK)):
+        j, first = divmod(2 * c * CHUNK, per_dev)
+        a = [a_ref[f:f + CHUNK, j].reshape(lanes, cols) for f in (first, first + CHUNK)]
+        wide_ref[c] = jnp.concatenate(a, axis=1)
+        wide_t_ref[c] = jnp.concatenate([m.T for m in a], axis=0)
+
+    masks, key_parts, w_parts = [], [], []
+
+    def slot_col(g, values):
         return jnp.concatenate(
             [
-                jnp.sum(jnp.where(m, values, 0.0), axis=2, keepdims=True).reshape(half_slots, 1)
-                for m in masks
+                jnp.sum(jnp.where(m, values, 0.0), axis=2, keepdims=True).reshape(near * rh, 1)
+                for m in masks[g]
             ],
             axis=0,
         )
 
-    keys = slot_col(key_in + 1.0)
-    w_slot = slot_col(w_in)
-    up_slot = lax.broadcasted_iota(i32, (slots, 1), 0) >= half_slots
+    for g in (0, 1):
+        wait_group(g, meta_in, recv_sem.at[0])
+        got = meta_in[g * near:(g + 1) * near]
+        code_in, key_in, w_in = [got[:, :, i * pairs:(i + 1) * pairs] for i in range(3)]
+        want = me * (2 * rh) + lax.broadcasted_iota(i32, (near, rh, pairs), 1)
+        masks.append([code_in.astype(i32) == want, code_in.astype(i32) == want + rh])
+        key_parts.append(slot_col(g, key_in + 1.0))
+        w_parts.append(slot_col(g, w_in))
+    keys = jnp.concatenate(key_parts, axis=0)
+    up_slot = lax.rem(lax.broadcasted_iota(i32, (slots, 1), 0), group_slots) >= near * rh
     local = jnp.where(up_slot, keys - sb, keys)
     local = jnp.where(keys > 0.0, local, 0.0)
+
+    def send_rows(stage, g, codes, more=()):
+        rows_out[stage, g * near:(g + 1) * near] = pack(codes).reshape(near, rh, cols)
+        rows = (lambda x: rows_out.at[stage, x], rows_in.at[stage], send_sem.at[stage + 1], recv_sem.at[stage + 1])
+        send_group(g, [*more, rows])
+        if g == 0:
+            rows_in[stage, 0] = rows_out[stage, 0]
+
+    def take_rows(stage, g):
+        wait_group(g, rows_in.at[stage], recv_sem.at[stage + 1])
+        return unpack(rows_in[stage, g * near:(g + 1) * near].reshape(near * rh, cols))
+
+    def zone_code(z):
+        return jnp.minimum(jnp.round(z * 32768.0), 65535.0).astype(i32)
+
+    prior = [None, None]
+    loads[0].wait()
+    old_parts = split(old_ref[...])
+    for g in (1, 0):
+        own = onehot(local[groups[g]] == lax.broadcasted_iota(i32, (group_slots, sb), 1).astype(f32) + 1.0)
+        own_ref[groups[g]] = own
+        picked = mm(own, old_parts)
+        prior[g] = picked[:, :cols] + picked[:, cols:]
+        send_rows(0, g, zone_code(prior[g]))
     keys_row = jnp.broadcast_to(keys, (slots, 128)).T[0:1]
     local_row = jnp.broadcast_to(local, (slots, 128)).T[0:1]
-    own_ref[...] = onehot(local == lax.broadcasted_iota(i32, (slots, sb), 1).astype(f32) + 1.0)
-
-    def send_rows(stage, codes):
-        rows_out[stage] = pack(codes).reshape(n, rh, cols)
-        exchange_start(
-            lambda e: rows_out.at[stage, e], rows_in.at[stage], send_sem.at[stage + 1], recv_sem.at[stage + 1]
-        )
-        rows_in[stage, n - 1] = rows_out[stage, n - 1]
-
-    def take_rows(stage):
-        wait_all(rows_in.at[stage], recv_sem.at[stage + 1])
-        return unpack(rows_in[stage].reshape(half_slots, cols))
-
-    def zone_code(z):
-        return jnp.minimum(jnp.round(z * 32768.0), 65535.0).astype(i32)
-
-    loads[0].wait()
-    prior = mm_split(own_ref[...], old_ref[...])
-    send_rows(0, zone_code(prior))
     loads[1].wait()
     high = mm_split(own_ref[...], high_ref[...])
+    high = [high[g] for g in groups]
     e_ref[...] = onehot(keys == keys_row)
-    w_wide = jnp.broadcast_to(w_slot, (slots, cols)).astype(bf16)
-    totals = mm(e_ref[...], w_wide)
-    step = 0.5 / (1.0 + totals)
-
+    w_wide = [jnp.broadcast_to(w, (group_slots, cols)).astype(bf16) for w in w_parts]
+    totals = mm(e_ref[...], jnp.concatenate(w_wide, axis=0))
+    totals = [totals[g] for g in groups]
+    step = [0.5 / (1.0 + t) for t in totals]
     for j in range(touched):
         at = slice(j * per_dev, (j + 1) * per_dev)
         lin_ref[at] = unit_ref[:, j, :].astype(f32) + mult_ref[:, j, :].astype(f32)
         base_ref[0, at] = dual_ref[:, j, :].astype(f32)
         base_ref[1, at] = demand_ref[:, j, :].astype(f32)
-    loads[2].wait()
+
+    def pick(stage):
+        near_rows = mm(g_ref[:, groups[0]], to_bytes(take_rows(stage, 0)))
+        return near_rows + mm(g_ref[:, groups[1]], to_bytes(take_rows(stage, 1)))
 
     def home(stage, which, dual):
         base = base_ref[0] - dual * base_ref[1]
         base = jnp.concatenate([base] * (128 // rb), axis=1)
-        x = mm(g_ref[...], to_bytes(take_rows(stage))).astype(bf16)
-        lanes = CHUNK * rb
-        diag = lax.broadcasted_iota(i32, (CHUNK, lanes), 0) == (
-            lax.broadcasted_iota(i32, (CHUNK, lanes), 1) // rb
+        x = pick(stage)
+        both_rows = 2 * CHUNK
+        diag = lax.rem(lax.broadcasted_iota(i32, (both_rows, lanes), 0), CHUNK) == (
+            lax.broadcasted_iota(i32, (both_rows, lanes), 1) // rb
         )
+        first_chunk = lax.broadcasted_iota(i32, (both_rows, cols), 0) < CHUNK
         pulled = []
-        for c in range(pairs // CHUNK):
-            j, first = divmod(c * CHUNK, per_dev)
-            a = a_ref[first:first + CHUNK, j].reshape(lanes, cols)
-            bc = base[c * CHUNK:(c + 1) * CHUNK]
-            bc = jnp.concatenate([bc] * (lanes // 128), axis=1)
-            xc = x[c * CHUNK:(c + 1) * CHUNK]
-            xc = jnp.concatenate([xc[:, :cols], xc[:, cols:]], axis=0)
-            r = lax.dot_general(xc, a, (((1,), (1,)), ((), ())), preferred_element_type=f32)
-            r = (r[:CHUNK] * 256.0 + r[CHUNK:]) * (dual / 32768.0)
+        for c in range(pairs // both_rows):
+            at = slice(c * both_rows, (c + 1) * both_rows)
+            bc = jnp.concatenate([base[at]] * (lanes // 128), axis=1)
+            xc = jnp.concatenate(
+                [
+                    jnp.concatenate([jnp.where(first_chunk, v, 0.0), jnp.where(first_chunk, 0.0, v)], axis=1)
+                    for v in (x[at, :cols], x[at, cols:])
+                ],
+                axis=0,
+            ).astype(bf16)
+            r = mm(xc, wide_t_ref[c])
+            r = (r[:both_rows] * 256.0 + r[both_rows:]) * (dual / 32768.0)
             inner = jnp.where(diag, r + bc, 0.0)
             hi = inner.astype(bf16)
             lo = (inner - hi.astype(f32)).astype(bf16)
-            g = mm(jnp.concatenate([hi, lo], axis=0), a)
-            pulled.append(g[:CHUNK] + g[CHUNK:])
+            g = mm(jnp.concatenate([hi, lo], axis=0), wide_ref[c])
+            g = g[:both_rows] + g[both_rows:]
+            pulled.append(jnp.where(first_chunk, g[:, :cols], g[:, cols:]))
         terms = w_col * (lin_ref[...] + jnp.concatenate(pulled, axis=0))
         peak = jnp.maximum(jnp.max(jnp.abs(terms), axis=1, keepdims=True), 1e-30)
         unit = peak * (1.0 / 32767.0)
         scale_out[which] = jnp.broadcast_to(unit, (pairs, 128)).T[0:1]
         codes = jnp.round(terms / unit) + 32768.0
         codes = jnp.clip(codes, 0.0, 65535.0).astype(i32)
-        exchange_start(lambda e: scale_out.at[which], scale_in.at[which], scale_send.at[which], scale_recv.at[which])
-        scale_in[which, n - 1] = scale_out[which]
-        placed = mm(gt_ref[...], to_bytes(codes))
-        placed = (placed[:, :cols] * 256.0 + placed[:, cols:]).astype(i32)
-        send_rows(stage + 1, placed)
+        scale_in[which, 0] = scale_out[which]
+        scale = (lambda x: scale_out.at[which], scale_in.at[which], scale_send.at[which], scale_recv.at[which])
+        codes = to_bytes(codes)
+        for g in (1, 0):
+            placed = mm(gt_ref[groups[g]], codes)
+            placed = (placed[:, :cols] * 256.0 + placed[:, cols:]).astype(i32)
+            send_rows(stage + 1, g, placed, [scale])
+
+    def terms_in(stage, which, g):
+        wait_group(g, scale_in.at[which], scale_recv.at[which])
+        unit = slot_col(g, scale_in[which, g * near:(g + 1) * near])
+        return (take_rows(stage, g) - 32768).astype(f32) * unit
 
     def gradient(stage, which):
-        wait_all(scale_in.at[which], scale_recv.at[which])
-        unit = slot_col(scale_in[which])
-        codes = take_rows(stage)
-        terms = (codes - 32768).astype(f32) * unit
-        return mm_split(e_ref[...], terms)
+        from_near = mm_split(e_ref[:, groups[0]], terms_in(stage, which, 0))
+        far = split(terms_in(stage, which, 1))
+
+        def total(g):
+            out = mm(e_ref[groups[g], groups[1]], far)
+            return from_near[groups[g]] + (out[:, :cols] + out[:, cols:])
+        return total
 
     home(0, 0, 0.5)
     eq_ref[...] = onehot(local == local_row)
-    zone_one = jnp.clip(prior - step * gradient(1, 0), 0.0, high)
-    send_rows(2, zone_code(zone_one))
+    grad = gradient(1, 0)
+    zone_one = [None, None]
+    for g in (1, 0):
+        zone_one[g] = jnp.clip(prior[g] - step[g] * grad(g), 0.0, high[g])
+        send_rows(2, g, zone_code(zone_one[g]))
     home(2, 1, 1.0)
     own_t_ref[...] = onehot(local_row == lax.broadcasted_iota(i32, (sb, slots), 0).astype(f32) + 1.0)
-    grad = gradient(3, 1) + totals * (zone_one - prior)
-    zone_two = jnp.clip(zone_one - step * grad, 0.0, high)
-    weighted = w_slot * zone_two
-    both = jnp.concatenate([split(weighted), w_wide], axis=1)
-    sums = mm(eq_ref[...], both)
-    fresh = (prior + (sums[:, :cols] + sums[:, cols:2 * cols])) / (1.0 + sums[:, 2 * cols:])
-    delta = jnp.round((zone_two - fresh + 2.0) * 16384.0)
-    send_rows(4, jnp.clip(delta, 0.0, 65535.0).astype(i32))
+    grad = gradient(3, 1)
+    zone_two, both = [None, None], [None, None]
+    for g in (1, 0):
+        pull = grad(g) + totals[g] * (zone_one[g] - prior[g])
+        zone_two[g] = jnp.clip(zone_one[g] - step[g] * pull, 0.0, high[g])
+        both[g] = jnp.concatenate([split(w_parts[g] * zone_two[g]), w_wide[g]], axis=1)
+    both = jnp.concatenate(both, axis=0)
+    for g in (1, 0):
+        sums = mm(eq_ref[groups[g]], both)
+        fresh = (prior[g] + (sums[:, :cols] + sums[:, cols:2 * cols])) / (1.0 + sums[:, 2 * cols:])
+        delta = jnp.round((zone_two[g] - fresh + 2.0) * 16384.0)
+        send_rows(4, g, jnp.clip(delta, 0.0, 65535.0).astype(i32))
     sums = mm(own_t_ref[...], both)
     fresh_ref[...] = (old_ref[...] + (sums[:, :cols] + sums[:, cols:2 * cols])) / (
         1.0 + sums[:, 2 * cols:]
     )
-    out = mm(g_ref[...], to_bytes(take_rows(4)))
+    out = pick(4)
     diff = (out[:, :cols] * 256.0 + out[:, cols:]) * (1.0 / 16384.0) - 2.0
     for j in range(touched):
         out_ref[:, j, :] = mult_ref[:, j, :].astype(f32) + diff[j * per_dev:(j + 1) * per_dev]
 
-    wait_all(meta_in, send_sem.at[0])
+    wait_sent(meta_in, send_sem.at[0])
     for stage in range(5):
-        wait_all(rows_in.at[stage], send_sem.at[stage + 1])
+        wait_sent(rows_in.at[stage], send_sem.at[stage + 1])
     for which in range(2):
-        wait_all(scale_in.at[which], scale_send.at[which])
+        wait_sent(scale_in.at[which], scale_send.at[which])
 
 
 def hand_on(fresh_in, updated_in, fresh_ref, updated_ref, sem):
@@ -314,14 +367,16 @@
             pltpu.VMEM((slots, sb), bf16),
             pltpu.VMEM((sb, slots), bf16),
             pltpu.VMEM(constraint.shape, bf16),
+            pltpu.VMEM((pairs // (2 * CHUNK), CHUNK * rb, 2 * cols), bf16),
+            pltpu.VMEM((pairs // (2 * CHUNK), 2 * cols, CHUNK * rb), bf16),
             pltpu.VMEM((pairs, cols), f32),
             pltpu.VMEM((2, pairs, rb), f32),
             pltpu.VMEM((sb, cols), f32),
             pltpu.VMEM((sb, cols), f32),
             pltpu.SemaphoreType.DMA((6,)),
-            pltpu.SemaphoreType.DMA((6,)),
+            pltpu.SemaphoreType.DMA((6, 2)),
             pltpu.SemaphoreType.DMA((2,)),
-            pltpu.SemaphoreType.DMA((2,)),
+            pltpu.SemaphoreType.DMA((2, 2)),
             pltpu.SemaphoreType.DMA((3,)),
         ],
         compiler_params=pltpu.CompilerParams(

time: 45.3 us -> 43.5 us (0.960)
  Pallas kernels: 44.5 us -> 42.6 us
    pallas_call x1, Pallas kernels: 42.8 us -> 40.9 us  [body(): pl.pallas_call(functools.partial(kernel, n, n_bund, rh, sb, rb), out_shap...]
where the time goes in v4:
time: 43.5 us; the launch traced here: 43.3 us
  Pallas kernels  42.6 us (98%)
  between operations  0.64 us (1%)
    pallas_call x1, Pallas kernels, body(): pl.pallas_call(functools.partial(kernel, n, n_bund, rh, sb, rb), out_shap...  40.9 us
    pallas_call x1, Pallas kernels, body(): pl.pallas_call(hand_on, out_shape=(jax.ShapeDtypeStruct(fresh.shape, f32)...  1.68 us

profile of v4, /device:TPU:0, one launch (start us, length us, event | category | flops | bytes accessed | tf_op | source)
XLA Modules:
  0.0 43.3 jit_solution(8314497385411861164)
XLA Ops:
  0.6 40.9 %shard_map.113 = (f32[512,128]{1,0:T(8,128)}, f32[64,2,128]{2,1,0:T(2,128)}) custom-call(s32[1,64]{1,0:T(1,128)} %bitcast.9, s32[2,64]{1,0:T(2,128)} %bitcast.8, bf16[1,64]{1,0:T(2,128)(2,1)} %bitcast.10, bf16[64,2,128]{2,1,0:T(2,128)(2,1)} %unit_ref.1, bf16[64,2,128]{2,1,0:T(2,128)(2,1)} %mult_ref.1, bf16[64,2,64]{2,1,0:T(2,128)(2,1)} %dual_ref.1, ...), custom_call_target="tpu_custom_call" | custom-call | tf_op jit(solution)/shard_map/pallas_call | solution.py:348
  41.6 1.7 %shard_map.114 = (f32[512,128]{1,0:T(8,128)}, f32[64,2,128]{2,1,0:T(2,128)}) custom-call(f32[512,128]{1,0:T(8,128)} %get-tuple-element.6.fresh_in, f32[64,2,128]{2,1,0:T(2,128)} %get-tuple-element.7.updated_in), custom_call_target="tpu_custom_call" | custom-call | tf_op jit(solution)/shard_map/pallas_call | solution.py:393
